TPU v7x, 32 devices: a whole 2x2x4 slice. The times are simulated.
32 devices in a mesh: row: 4 (over y, core), col: 8 (over z, x).
Axes of the slice: x: 2, y: 2, z: 4, core: 2. Of those that a mesh axis runs over, the one named last changes fastest.
Arguments:
- fock: bfloat16 [32768, 8, 4096], P('row', 'col'), may hold values from -6 to 6
- lmo_coef: bfloat16 [32768, 1024], P(('row', 'col')), may hold values from -0.078125 to 0.078125
- three_index: bfloat16 [32768, 512], P(('row', 'col')), may hold values from -6 to 6
- rotation: bfloat16 [8, 4, 1024, 512], P('col', 'row'), may hold values from -0.1875 to 0.1875
- lmo_ids: int32 [8, 4], replicated, may hold values from 0 to 31, as said below
- domains: int32 [32, 8], replicated, may hold values from -1 to 255, as said below
Outputs:
- proj_fock: float32 [8, 4, 512, 512], P('col', 'row')
- three_rot: bfloat16 [8, 4, 512, 512], P('col', 'row')
Inputs may be any that keep to these rules, and one draw needn't show every extreme that they name: `lmo_ids`: every LMO number appears exactly once; row o lists the 4 LMOs owned by column set o. `domains`: entry k of a list is -1 or a block of row panel k // 2; entry 0 is never -1. The present blocks of one list lie in distinct column sets. For one owner o and one entry k, the blocks of the lists of lmo_ids[o, j] over all j lie in distinct column sets; for one j and one entry k, those of lmo_ids[o, j] over all o do too.
All inputs are finite; a program needn't handle non-finite values.
Results may differ from a plain program's by a relative error of at most 0.02.
Values may be sent and summed in bfloat16 or wider, within the bound.
A program may use at most 320 MiB of HBM per device.

v0:
```python
import jax
import jax.numpy as jnp
from jax import lax
from jax.sharding import PartitionSpec as P

BLK = 128


def locate(blocks, dev_blocks, num_sets):
    present = blocks >= 0
    clipped = jnp.maximum(blocks, 0)
    flat_dev = clipped // dev_blocks
    return (present, flat_dev % num_sets, flat_dev // num_sets, clipped % dev_blocks)


def body(fock, lmo_coef, three_index, rotation, lmo_ids, domains):
    num_panels = lax.axis_size("row")
    num_sets = lax.axis_size("col")
    my_row = lax.axis_index("row")
    my_col = lax.axis_index("col")
    dev_rows = lmo_coef.shape[0]
    occ_width = lmo_coef.shape[1]
    dev_blocks = dev_rows // BLK
    dom_blocks = domains.shape[1]
    per_panel = dom_blocks // num_panels
    dev_lmos = rotation.shape[1]
    dom_width = dom_blocks * BLK
    panel_fock = fock[:, 0, :]
    gathered = lax.all_gather(lmo_coef, "row", axis=0, tiled=True)
    fock_coef = lax.psum_scatter(
        jnp.dot(panel_fock, gathered, preferred_element_type=jnp.float32).astype(jnp.bfloat16),
        "col",
        scatter_dimension=0,
        tiled=True,
    ).astype(jnp.float32)
    occ_term = jnp.einsum(
        "ri,rj->ij", lmo_coef, fock_coef.astype(jnp.bfloat16), preferred_element_type=jnp.float32
    )
    occ_fock = lax.psum(occ_term, ("row", "col"))
    correction = jnp.dot(
        lmo_coef, occ_fock.astype(jnp.bfloat16), preferred_element_type=jnp.float32
    )
    proj_rows = (fock_coef - 0.5 * correction).astype(jnp.bfloat16)
    all_rows = jnp.concatenate([lmo_coef, proj_rows, three_index], axis=1)
    row_width = all_rows.shape[1]
    row_blocks = all_rows.reshape(dev_blocks, BLK, row_width)
    fock_tiles = panel_fock.reshape(num_sets * dev_blocks, BLK, num_panels * dev_blocks, BLK)
    owner_doms = jnp.take(domains, lmo_ids, axis=0)
    present, col_set, panel_id, sub_block = locate(owner_doms, dev_blocks, num_sets)
    row_tile = col_set * dev_blocks + sub_block
    col_tile = panel_id * dev_blocks + sub_block
    holds_col = present & (col_set == my_col)
    my_col_tile = jnp.sum(jnp.where(holds_col, col_tile, 0), axis=2)
    has_col = jnp.any(holds_col, axis=2)
    sub_range = jnp.arange(dev_blocks, dtype=jnp.int32)
    set_range = jnp.arange(num_sets, dtype=jnp.int32)
    slot_start = my_row * per_panel
    mine_slot = lax.dynamic_slice_in_dim(holds_col, slot_start, per_panel, 2)
    sub_slot = lax.dynamic_slice_in_dim(sub_block, slot_start, per_panel, 2)
    row_slot = lax.dynamic_slice_in_dim(row_tile, slot_start, per_panel, 2)
    live_slot = lax.dynamic_slice_in_dim(present, slot_start, per_panel, 2) & has_col[:, :, None]
    owner_present = lax.dynamic_index_in_dim(present, my_col, 0, keepdims=False)
    owner_sets = lax.dynamic_index_in_dim(col_set, my_col, 0, keepdims=False)
    pick_rows = (mine_slot[..., None] & (sub_slot[..., None] == sub_range)).astype(jnp.bfloat16)
    rows_out = jnp.einsum(
        "ojps,sbw->opbw", pick_rows, row_blocks, preferred_element_type=jnp.float32
    ).astype(jnp.bfloat16)
    tiles_out = fock_tiles[row_slot, :, my_col_tile[:, :, None], :]
    tiles_out = jnp.where(live_slot[..., None, None], tiles_out, jnp.zeros_like(tiles_out))
    got_rows, got_tiles = (
        lax.all_to_all(rows_out, "col", split_axis=0, concat_axis=0, tiled=True),
        lax.all_to_all(tiles_out, "col", split_axis=0, concat_axis=0, tiled=True),
    )
    source = ((owner_sets[..., None] == set_range) & owner_present[..., None]).astype(jnp.bfloat16)
    source_slot = lax.dynamic_slice_in_dim(source, slot_start, per_panel, 1)
    source_slot = source_slot.reshape(num_panels, dev_lmos, per_panel, num_sets)
    strip_rows = jnp.einsum(
        "rdps,spbw->drpbw", source_slot, got_rows, preferred_element_type=jnp.float32
    ).astype(jnp.bfloat16)
    source_all = source.reshape(num_panels, dev_lmos, dom_blocks, num_sets)
    tiles_in = got_tiles.reshape(num_sets, num_panels, dev_lmos, per_panel, BLK, BLK)
    strip_fock = jnp.einsum(
        "rdks,srdpab->drpakb", source_all, tiles_in, preferred_element_type=jnp.float32
    ).astype(jnp.bfloat16)
    strip_fock = strip_fock.reshape(dev_lmos, num_panels, per_panel, BLK, dom_width)
    fin_rows, fin_fock = (
        lax.all_to_all(strip_rows, "row", split_axis=1, concat_axis=1, tiled=True),
        lax.all_to_all(strip_fock, "row", split_axis=1, concat_axis=1, tiled=True),
    )
    fin_rows = fin_rows.reshape(dev_lmos, dom_width, row_width)
    fin_fock = fin_fock.reshape(dev_lmos, dom_width, dom_width)
    slot_rot = rotation[0]
    coef_dom = fin_rows[:, :, :occ_width]
    proj_dom = fin_rows[:, :, occ_width : 2 * occ_width]
    three_dom = fin_rows[:, :, 2 * occ_width :]
    fock_half = jnp.einsum(
        "dxy,dyn->dxn", fin_fock, slot_rot, preferred_element_type=jnp.float32
    ).astype(jnp.bfloat16)
    fock_rot = jnp.einsum("dxm,dxn->dmn", slot_rot, fock_half, preferred_element_type=jnp.float32)
    coef_rot = jnp.einsum(
        "dxm,dxi->dmi", slot_rot, coef_dom, preferred_element_type=jnp.float32
    ).astype(jnp.bfloat16)
    proj_rot = jnp.einsum(
        "dxm,dxi->dmi", slot_rot, proj_dom, preferred_element_type=jnp.float32
    ).astype(jnp.bfloat16)
    proj_fock = fock_rot - jnp.einsum(
        "dmi,dni->dmn", coef_rot, proj_rot, preferred_element_type=jnp.float32
    )
    proj_fock = proj_fock - jnp.einsum(
        "dmi,dni->dmn", proj_rot, coef_rot, preferred_element_type=jnp.float32
    )
    three_rot = jnp.einsum(
        "dxm,dxu->dmu", slot_rot, three_dom, preferred_element_type=jnp.float32
    ).astype(jnp.bfloat16)
    return (proj_fock[None], three_rot[None])


def solution(mesh):
    placed = (
        P("row", "col", None),
        P(("row", "col"), None),
        P(("row", "col"), None),
        P("col", "row", None, None),
        P(),
        P(),
    )
    return jax.shard_map(
        body,
        mesh=mesh,
        in_specs=placed,
        out_specs=(P("col", "row", None, None), P("col", "row", None, None)),
        check_vma=False,
    )
```

profile of v0, /device:TPU:0, one launch (start us, length us, event | category | flops | bytes accessed | tf_op | source)
XLA Modules:
  0.0 936.4 jit_solution(13196458141406307616)
XLA Ops:
  8.0 62.6 %all-gather.2.cloned.1.call-done = bf16[4096,1024]{1,0:T(8,128)(2,1)} async-done(((bf16[1024,1024]{1,0:T(8,128)(2,1)}), bf16[4096,1024]{1,0:T(8,128)(2,1)}) %all-gather.2.cloned.1.call-update) | async-done | bytes 8388624 | tf_op jit(solution)/shard_map/all_gather | solution.py:29
  70.6 77.6 %fusion.2 = bf16[8192,1024]{1,0:T(8,128)(2,1)} fusion(bf16[4096,1024]{1,0:T(8,128)(2,1)} %all-gather.2.cloned.1.call-done, bf16[8192,1,4096]{2,0,1:T(8,128)(2,1)} %param.6), kind=kOutput, calls=%fused_computation.4 | convolution fusion | flops 68727865344 | bytes 92274688 | tf_op jit(solution)/shard_map/dot_general | solution.py:31
  148.2 45.4 %copy.110 = bf16[1024,8,32,128]{3,2,1,0:T(8,128)(2,1)} copy(bf16[1024,8,32,128]{3,1,2,0:T(8,128)(2,1)} %bitcast.37) | data formatting | bytes 134217728
  193.6 45.2 %copy.85 = bf16[64,128,32,128]{3,1,2,0:T(8,128)(2,1)} copy(bf16[64,128,32,128]{3,2,1,0:T(8,128)(2,1)} %bitcast.39) | data formatting | bytes 134217728 | tf_op jit(solution)/shard_map/reshape;squeeze | solution.py:47
  240.7 3.6 gather_fusion.1
  244.4 3.3 broadcast_select_fusion
  247.8 5.2 all-to-all-start
  253.4 217.9 %reduce-scatter.2.cloned.1.call-done = bf16[1024,1024]{1,0:T(8,128)(2,1)} async-done(((bf16[8192,1024]{1,0:T(8,128)(2,1)}), bf16[1024,1024]{1,0:T(8,128)(2,1)}) %reduce-scatter.2.cloned.1.call-update) | async-done | bytes 2097168 | tf_op jit(solution)/shard_map/reduce_scatter | solution.py:30
  471.3 5.9 convolution_bitcast_fusion
  477.2 91.4 %all-reduce.1 = bf16[1024,1024]{0,1:T(8,128)(2,1)} all-reduce(f32[1024,1024]{0,1:T(8,128)} %convolution_bitcast_fusion), channel_id=1, replica_groups=mesh['row'=4,'col'=8] {'row','col'}, use_global_device_ids=true, to_apply=%region_4.5 | all-reduce | flops 1048576 | bytes 6291456 | tf_op jit(solution)/shard_map/psum | solution.py:39
  568.6 4.7 fusion.15
  573.8 6.0 convolution_convert_fusion
  579.8 11.3 %copy.95 = bf16[8,2,128,2560]{3,2,1,0:T(8,128)(2,1)} copy(bf16[8,2,128,2560]{3,0,2,1:T(8,128)(2,1)} %convolution_convert_fusion) | data formatting | bytes 20971520 | tf_op jit(solution)/shard_map/convert_element_type | solution.py:67
  591.1 5.2 all-to-all-start.2
  596.6 2.9 convert_bitcast_fusion
  601.8 222.3 %all-to-all-done.2 = bf16[8,2,128,2560]{3,2,1,0:T(8,128)(2,1)} async-done(((bf16[8,2,128,2560]{3,2,1,0:T(8,128)(2,1)}), bf16[8,2,128,2560]{3,2,1,0:T(8,128)(2,1)}, u32[]{:S(2)}, u32[]{:S(2)}) %all-to-all-start.2) | async-done | bytes 10485792 | tf_op jit(solution)/shard_map/all_to_all | solution.py:71
  824.1 3.8 all-to-all-start.1
  828.0 10.9 %fusion.12 = bf16[1,4,2,128,2560]{4,1,3,2,0:T(4,128)(2,1)S(1)} fusion(bf16[8,2,128,2560]{3,2,1,0:T(8,128)(2,1)} %all-to-all-done.2, pred[4,8,8]{2,0,1:T(4,128)(4,1)S(1)} %fusion.45, s32[]{:T(128)S(6)} %select_n.62), kind=kOutput, calls=%fused_computation.12 | convolution fusion | flops 44564480 | bytes 15729668 | tf_op jit(solution)/shard_map/rdps,spbw->drpbw/dot_general | solution.py:77
  838.9 3.3 copy.97
  842.2 11.2 %all-to-all-done.1 = bf16[1,4,2,128,1024]{4,3,2,0,1:T(8,128)(2,1)S(1)} async-done(((bf16[1,4,2,128,1024]{4,3,2,0,1:T(8,128)(2,1)}), bf16[1,4,2,128,1024]{4,3,2,0,1:T(8,128)(2,1)S(1)}, u32[]{:S(2)}, u32[]{:S(2)}) %all-to-all-start.1) | async-done | bytes 2097184 | tf_op jit(solution)/shard_map/all_to_all | solution.py:88
  853.3 5.1 all-to-all-start.3
  861.2 56.7 %all-to-all-done.3 = bf16[1,4,2,128,2560]{4,3,2,0,1:T(8,128)(2,1)} async-done(((bf16[1,4,2,128,2560]{4,3,2,0,1:T(8,128)(2,1)}), bf16[1,4,2,128,2560]{4,3,2,0,1:T(8,128)(2,1)}, u32[]{:S(2)}, u32[]{:S(2)}) %all-to-all-start.3) | async-done | bytes 5242912 | tf_op jit(solution)/shard_map/all_to_all | solution.py:87
  917.9 2.9 fusion.23
  920.8 3.0 fusion.24
  (52 shorter events, 14.9 us)
Async XLA Ops:
  7.2 851.3 %copy-start = (bf16[1,1,1024,512]{3,2,1,0:T(8,128)(2,1)S(1)}, bf16[1,1,1024,512]{3,2,1,0:T(8,128)(2,1)}, u32[]{:S(2)}) copy-start(bf16[1,1,1024,512]{3,2,1,0:T(8,128)(2,1)} %param.9) | copy-start | bytes 3145732
  7.2 63.4 %all-gather.2.cloned.1.call-start = ((), (), s32[]{:S(2)}) async-start(), calls=%async_computation.5 | async-start | bytes 10485760 | tf_op jit(solution)/shard_map/all_gather | solution.py:29
  7.9 463.4 %reduce-scatter.2.cloned.1.call-start = ((), (), s32[]{:S(2)}) async-start(), calls=%async_computation.6 | async-start | bytes 18874368 | tf_op jit(solution)/shard_map/reduce_scatter | solution.py:30
  193.6 45.2 %copy-start.4 = (s32[32,8]{0,1:T(8,128)S(1)}, s32[32,8]{0,1:T(8,128)}, u32[]{:S(2)}) copy-start(s32[32,8]{0,1:T(8,128)} %param.11) | copy-start | bytes 3076
  193.6 45.2 %copy-start.5 = (s32[8,4]{0,1:T(4,128)S(1)}, s32[8,4]{0,1:T(4,128)}, u32[]{:S(2)}) copy-start(s32[8,4]{0,1:T(4,128)} %param.10) | copy-start | bytes 388
  244.4 226.9 %copy-start.1 = (bf16[1024,1024]{1,0:T(8,128)(2,1)S(1)}, bf16[1024,1024]{1,0:T(8,128)(2,1)}, u32[]{:S(2)}) copy-start(bf16[1024,1024]{1,0:T(8,128)(2,1)} %param.7) | copy-start | bytes 6291460
  247.8 343.4 %all-to-all-start = ((bf16[8,4,2,128,128]{4,3,2,1,0:T(8,128)(2,1)}), bf16[8,4,2,128,128]{4,3,2,1,0:T(8,128)(2,1)}, u32[]{:S(2)}, u32[]{:S(2)}) async-start(bf16[8,4,2,128,128]{4,3,2,1,0:T(8,128)(2,1)} %broadcast_select_fusion), calls=%async_computation | async-start | bytes 4194304 | tf_op jit(solution)/shard_map/all_to_all | solution.py:72
  568.6 4.7 copy-start.2
  591.1 233.0 %all-to-all-start.2 = ((bf16[8,2,128,2560]{3,2,1,0:T(8,128)(2,1)}), bf16[8,2,128,2560]{3,2,1,0:T(8,128)(2,1)}, u32[]{:S(2)}, u32[]{:S(2)}) async-start(bf16[8,2,128,2560]{3,2,1,0:T(8,128)(2,1)} %copy.95), calls=%async_computation.3 | async-start | bytes 20971520 | tf_op jit(solution)/shard_map/all_to_all | solution.py:71
  824.1 29.3 %all-to-all-start.1 = ((bf16[1,4,2,128,1024]{4,3,2,0,1:T(8,128)(2,1)}), bf16[1,4,2,128,1024]{4,3,2,0,1:T(8,128)(2,1)S(1)}, u32[]{:S(2)}, u32[]{:S(2)}) async-start(bf16[1,4,2,128,1024]{4,3,2,0,1:T(8,128)(2,1)} %bitcast.101), calls=%async_computation.1 | async-start | bytes 4194304 | tf_op jit(solution)/shard_map/all_to_all | solution.py:88
  853.3 64.6 %all-to-all-start.3 = ((bf16[1,4,2,128,2560]{4,3,2,0,1:T(8,128)(2,1)}), bf16[1,4,2,128,2560]{4,3,2,0,1:T(8,128)(2,1)}, u32[]{:S(2)}, u32[]{:S(2)}) async-start(bf16[1,4,2,128,2560]{4,3,2,0,1:T(8,128)(2,1)} %copy.97), calls=%async_computation.4 | async-start | bytes 10485760 | tf_op jit(solution)/shard_map/all_to_all | solution.py:87
  920.8 4.9 copy-start.3
Sparse Core Ops, SparseCore 0:
  9.6 60.9 all-gather.1
  148.3 322.9 reduce-scatter.1
where the time goes:
time: 937 us; the launch traced here: 936 us
  waiting for transfers between devices  571 us (61%)
  matrix products  120 us (13%)
  local copies, waits for them, and re-layouts  115 us (12%)
  blocking collectives  91.4 us (10%)
  starting transfers between devices  19.4 us (2%)
  between operations  14.3 us (2%)
    all_to_all x1, waiting for transfers between devices, body(): lax.all_to_all(rows_out, 'col', split_axis=0, concat_axis=0, tiled=True)  222 us
    reduce_scatter x1, waiting for transfers between devices, body(): lax.psum_scatter(jnp.dot(panel_fock, gathered, preferred_element_type=jnp...  218 us
    psum x1, blocking collectives, body(): occ_fock = lax.psum(occ_term, ('row', 'col'))  91.4 us
    dot_general x1, matrix products, body(): jnp.dot(panel_fock, gathered, preferred_element_type=jnp.float32)  77.6 us
    all_gather x1, waiting for transfers between devices, body(): gathered = lax.all_gather(lmo_coef, 'row', axis=0, tiled=True)  62.6 us
    all_to_all x1, waiting for transfers between devices, body(): lax.all_to_all(strip_rows, 'row', split_axis=1, concat_axis=1, tiled=True)  56.7 us
    unnamed x17, local copies, waits for them, and re-layouts  47.9 us
    another operation x1, local copies, waits for them, and re-layouts, body(): panel_fock.reshape(num_sets * dev_blocks, BLK, num_panels * dev_blocks, BLK)  45.2 us
  transfers between devices with their start and end apart: 6, of which 5 were waited for; matrix products, arithmetic and copies ran while one was open for 16% of the time, Pallas kernels for 0%

commit v1 on v0

v1 whole, which is shorter than its diff:
```python
import functools

import jax
import jax.numpy as jnp
from jax import lax
from jax.experimental import pallas as pl
from jax.experimental.pallas import tpu as pltpu
from jax.sharding import PartitionSpec as P

BLK = 128


def pick_kernel(count, width, row_ref, col_ref, src_ref, out_ref, sems):
    def copy(i):
        rows = pl.ds(pl.multiple_of(row_ref[i] * BLK, BLK), BLK)
        cols = pl.ds(pl.multiple_of(col_ref[i] * width, BLK), width)
        return pltpu.make_async_copy(src_ref.at[rows, cols], out_ref.at[i], sems.at[i])

    @pl.loop(0, count)
    def _(i):
        copy(i).start()

    @pl.loop(0, count)
    def _(i):
        copy(i).wait()


def pick(src, rows, cols=None, width=None):
    rows = rows.reshape(-1).astype(jnp.int32)
    count = rows.shape[0]
    width = width or src.shape[1]
    cols = jnp.zeros_like(rows) if cols is None else cols.reshape(-1).astype(jnp.int32)
    return pl.pallas_call(
        functools.partial(pick_kernel, count, width),
        out_shape=jax.ShapeDtypeStruct((count, BLK, width), src.dtype),
        in_specs=[
            pl.BlockSpec(memory_space=pltpu.SMEM),
            pl.BlockSpec(memory_space=pltpu.SMEM),
            pl.BlockSpec(memory_space=pl.ANY),
        ],
        out_specs=pl.BlockSpec(memory_space=pltpu.VMEM),
        scratch_shapes=[pltpu.SemaphoreType.DMA((count,))],
        compiler_params=pltpu.CompilerParams(vmem_limit_bytes=16 << 20),
        cost_estimate=pl.CostEstimate(
            flops=0, bytes_accessed=2 * count * BLK * width * 2, transcendentals=0
        ),
    )(rows, cols, src)


def dot32(a, b):
    return jnp.dot(a, b, preferred_element_type=jnp.float32)


def swap(x, axis):
    return lax.all_to_all(x, axis, split_axis=0, concat_axis=0, tiled=True)


def reduce_sets(panel_fock, gathered, dev_rows, num_sets, my_col):
    if num_sets != 8:
        part = dot32(panel_fock, gathered).astype(jnp.bfloat16)
        return lax.psum_scatter(part, "col", scatter_dimension=0, tiled=True).astype(jnp.float32)
    zi, xi = my_col // 2, my_col % 2
    order = jnp.array([[3, 2, 1, 0], [3, 2, 0, 1], [0, 1, 3, 2], [0, 1, 2, 3]], jnp.int32)
    mine = lax.dynamic_index_in_dim(order, zi, 0, keepdims=False)
    pairs = [(c, c ^ 1) for c in range(8)]

    def part(dest_z, dest_x):
        rows = lax.dynamic_slice_in_dim(panel_fock, (dest_z * 2 + dest_x) * dev_rows, dev_rows, 0)
        return dot32(rows, gathered)

    sums = []
    for n in range(4):
        away = part(mine[n], 1 - xi).astype(jnp.bfloat16)
        came = lax.ppermute(away, "col", pairs)
        sums.append(part(mine[n], xi) + came.astype(jnp.float32))

    def hop(x, step, up):
        if up:
            perm = [(z * 2 + x_, z * 2 + 2 + x_) for z in range(step + 1) for x_ in range(2)]
        else:
            perm = [(z * 2 + x_, z * 2 - 2 + x_) for z in range(3 - step, 4) for x_ in range(2)]
        return lax.ppermute(x.astype(jnp.bfloat16), "col", perm).astype(jnp.float32)

    up = hop(sums[0], 0, True)
    down = hop(sums[0], 0, False)
    up = hop(jnp.where(zi == 0, sums[1], sums[0]) + up, 1, True)
    down = hop(jnp.where(zi == 3, sums[1], sums[0]) + down, 1, False)
    up_own = jnp.where(zi == 1, sums[1], sums[2])
    down_own = jnp.where(zi == 2, sums[1], sums[2])
    up = hop(up_own + up, 2, True)
    down = hop(down_own + down, 2, False)
    return sums[3] + up + down


def body(fock, lmo_coef, three_index, rotation, lmo_ids, domains):
    num_panels = lax.axis_size("row")
    num_sets = lax.axis_size("col")
    my_row = lax.axis_index("row")
    my_col = lax.axis_index("col")
    dev_rows = lmo_coef.shape[0]
    dev_blocks = dev_rows // BLK
    dom_blocks = domains.shape[1]
    per_panel = dom_blocks // num_panels
    dom_width = dom_blocks * BLK
    panel_fock = fock[:, 0, :]
    slot_rot = rotation[0, 0]

    lists = jnp.take(domains, lmo_ids, axis=0)
    present = lists >= 0
    clipped = jnp.maximum(lists, 0)
    flat_dev = clipped // dev_blocks
    col_set = flat_dev % num_sets
    panel_id = flat_dev // num_sets
    sub_block = clipped % dev_blocks
    col_tile = panel_id * dev_blocks + sub_block
    row_tile = col_set * dev_blocks + sub_block
    here = present & (col_set == my_col)

    def panel(x):
        return lax.dynamic_slice_in_dim(x, my_row * per_panel, per_panel, 2)

    row_pick = jnp.sum(jnp.where(panel(here), panel(sub_block), 0), axis=0)
    here_row = lax.dynamic_index_in_dim(here, my_row, 1, keepdims=False)
    tile_row = lax.dynamic_index_in_dim(col_tile, my_row, 1, keepdims=False)
    entry = jnp.arange(dom_blocks, dtype=jnp.int32)
    set_pick = jnp.sum(jnp.where(here_row, entry, 0), axis=1)
    coef_pick = jnp.sum(jnp.where(here_row, tile_row, 0), axis=1)
    my_col_tile = jnp.sum(jnp.where(here, col_tile, 0), axis=2)
    tile_rows = jnp.transpose(panel(row_tile), (1, 0, 2))
    tile_cols = jnp.broadcast_to(my_col_tile.T[:, :, None], tile_rows.shape)
    own_set = col_set[my_col, my_row]
    own_present = present[my_col, my_row]
    match = own_present & (own_set == jnp.arange(num_sets, dtype=jnp.int32)[:, None])
    own_entry = jnp.sum(jnp.where(match, entry, 0), axis=1)

    gathered = lax.all_gather(lmo_coef, "row", axis=0, tiled=True)

    tiles = pick(panel_fock, tile_rows, tile_cols, BLK)
    tiles = swap(tiles.reshape(num_panels, num_sets, per_panel, BLK, BLK), "row")
    tiles = jnp.transpose(tiles, (1, 0, 2, 3, 4)).reshape(num_sets, dom_blocks, BLK, BLK)
    tiles = swap(tiles, "col")

    three_rows = swap(pick(three_index, row_pick), "row")
    three_dom = swap(pick(three_rows.reshape(dom_width, -1), set_pick), "col")
    coef_dom = swap(pick(gathered, coef_pick), "col")

    fock_coef = reduce_sets(panel_fock, gathered, dev_rows, num_sets, my_col)
    coef_b = fock_coef.astype(jnp.bfloat16)

    occ_term = jnp.einsum("ri,rj->ij", lmo_coef, coef_b, preferred_element_type=jnp.float32)
    occ_part = lax.psum_scatter(occ_term, ("row", "col"), scatter_dimension=0, tiled=True)
    occ_b = lax.all_gather(occ_part.astype(jnp.bfloat16), ("row", "col"), axis=0, tiled=True)

    fc_rows = swap(pick(coef_b, row_pick), "row")
    fc_dom = swap(pick(fc_rows.reshape(dom_width, -1), set_pick), "col")

    rot_set = pick(slot_rot, own_entry)
    rot_set = jnp.where(jnp.any(match, axis=1)[:, None, None], rot_set, jnp.zeros_like(rot_set))
    rot_set = rot_set.reshape(num_sets * BLK, -1)
    rot_live = jnp.where(jnp.repeat(own_present, BLK)[:, None], slot_rot, jnp.zeros_like(slot_rot))

    def rotate(dom, rot):
        dom = dom.reshape(rot.shape[0], -1)
        return jnp.einsum("xm,xi->mi", rot, dom, preferred_element_type=jnp.float32)

    three_rot = rotate(three_dom, rot_set).astype(jnp.bfloat16)
    coef_rot = rotate(coef_dom, rot_set).astype(jnp.bfloat16)
    dom_fock = jnp.transpose(tiles, (1, 2, 0, 3)).reshape(dom_width, num_sets * BLK)
    fock_half = dot32(dom_fock, rot_set).astype(jnp.bfloat16)
    fock_rot = rotate(fock_half, rot_live)
    proj_rot = (rotate(fc_dom, rot_set) - 0.5 * dot32(coef_rot, occ_b)).astype(jnp.bfloat16)
    cross = jnp.einsum("mi,ni->mn", coef_rot, proj_rot, preferred_element_type=jnp.float32)
    proj_fock = fock_rot - cross - cross.T
    return (proj_fock[None, None], three_rot[None, None])


def solution(mesh):
    placed = (
        P("row", "col", None),
        P(("row", "col"), None),
        P(("row", "col"), None),
        P("col", "row", None, None),
        P(),
        P(),
    )
    return jax.shard_map(
        body,
        mesh=mesh,
        in_specs=placed,
        out_specs=(P("col", "row", None, None), P("col", "row", None, None)),
        check_vma=False,
    )
```

time: 937 us -> 633 us (0.68)
  waiting for transfers between devices: 571 us -> 344 us
  blocking collectives: 91.4 us -> 0 us
  local copies, waits for them, and re-layouts: 115 us -> 24.9 us
  starting transfers between devices: 19.4 us -> 63.4 us
  other arithmetic: 4.9 us -> 28.2 us
  Pallas kernels: 0 us -> 16.7 us
  matrix products: 120 us -> 130 us
    all_to_all x4 -> x7, waiting for transfers between devices: 290 us -> 73.4 us  [swap(): return lax.all_to_all(x, axis, split_axis=0, concat_axis=0, tiled=True)]
    reduce_scatter x1, waiting for transfers between devices: 218 us -> 82.9 us  [body(): lax.psum_scatter(occ_term, ('row', 'col'), scatter_dimension=0, tiled=True)]
    psum x1 -> x0, blocking collectives: 91.4 us -> none  [body(): occ_fock = lax.psum(occ_term, ('row', 'col'))]
    ppermute x0 -> x10, waiting for transfers between devices: none -> 73.1 us  [the longest x6 53.6 us: hop(): return lax.ppermute(x.astype(jnp.bfloat16), 'col', perm).astype(jnp.float32)]
    all_gather x0 -> x1, waiting for transfers between devices: none -> 57.3 us  [body(): lax.all_gather(occ_part.astype(jnp.bfloat16), ('row', 'col'), axis=0, til...]
    another operation x1, local copies, waits for them, and re-layouts: 45.2 us -> 0.01 us  [body(): panel_fock.reshape(num_sets * dev_blocks, BLK, num_panels * dev_blocks, BLK)]
    unnamed x17 -> x28, local copies, waits for them, and re-layouts: 47.9 us -> 12.3 us
    ppermute x0 -> x10, starting transfers between devices: none -> 32.3 us  [the longest x6 27.3 us: hop(): return lax.ppermute(x.astype(jnp.bfloat16), 'col', perm).astype(jnp.float32)]
  transfers between devices with their start and end apart: 6 -> 20, of which waited for: 5 -> 10; matrix products, arithmetic and copies ran while one was open for 16% -> 24% of each run, Pallas kernels for 0% -> 3%
where the time goes in v1:
time: 633 us; the launch traced here: 624 us
  waiting for transfers between devices  344 us (54%)
  matrix products  130 us (21%)
  starting transfers between devices  63.4 us (10%)
  other arithmetic  28.2 us (4%)
  local copies, waits for them, and re-layouts  24.9 us (4%)
  between operations  17 us (3%)
  Pallas kernels  16.7 us (3%)
    dot_general x9, matrix products, dot32(): return jnp.dot(a, b, preferred_element_type=jnp.float32)  111 us
    reduce_scatter x1, waiting for transfers between devices, body(): lax.psum_scatter(occ_term, ('row', 'col'), scatter_dimension=0, tiled=True)  82.9 us
    all_to_all x7, waiting for transfers between devices, swap(): return lax.all_to_all(x, axis, split_axis=0, concat_axis=0, tiled=True)  73.4 us
    all_gather x1, waiting for transfers between devices, body(): lax.all_gather(occ_part.astype(jnp.bfloat16), ('row', 'col'), axis=0, til...  57.3 us
    all_gather x1, waiting for transfers between devices, body(): gathered = lax.all_gather(lmo_coef, 'row', axis=0, tiled=True)  57.1 us
    ppermute x6, waiting for transfers between devices, hop(): return lax.ppermute(x.astype(jnp.bfloat16), 'col', perm).astype(jnp.float32)  53.6 us
    all_to_all x7, starting transfers between devices, swap(): return lax.all_to_all(x, axis, split_axis=0, concat_axis=0, tiled=True)  30.8 us
    ppermute x6, starting transfers between devices, hop(): return lax.ppermute(x.astype(jnp.bfloat16), 'col', perm).astype(jnp.float32)  27.3 us
  transfers between devices with their start and end apart: 20, of which 10 were waited for; matrix products, arithmetic and copies ran while one was open for 24% of the time, Pallas kernels for 3%

profile of v1, /device:TPU:0, one launch (start us, length us, event | category | flops | bytes accessed | tf_op | source)
XLA Modules:
  0.0 624.5 jit_solution(1723869409373829201)
XLA Ops:
  13.5 57.1 %all-gather.3.cloned.1.call-done.src_ref = bf16[4096,1024]{1,0:T(8,128)(2,1)} async-done(((bf16[1024,1024]{1,0:T(8,128)(2,1)}), bf16[4096,1024]{1,0:T(8,128)(2,1)}) %all-gather.3.cloned.1.call-update) | async-done | bytes 8388624 | tf_op jit(solution)/shard_map/all_gather | solution.py:136
  70.6 14.7 %fusion.37 = bf16[1024,1024]{1,0:T(8,128)(2,1)} fusion(bf16[4096,1024]{1,0:T(8,128)(2,1)} %all-gather.3.cloned.1.call-done.src_ref, bf16[8192,1,4096]{2,0,1:T(8,128)(2,1)} %param.7, s32[]{:T(128)S(6)} %select_n.165), kind=kOutput, calls=%fused_computation.43 | convolution fusion | flops 8590983168 | bytes 18874372 | tf_op jit(solution)/shard_map/dot_general | solution.py:51
  100.1 13.8 %fusion.31 = bf16[1024,1024]{1,0:T(8,128)(2,1)S(1)} fusion(bf16[4096,1024]{1,0:T(8,128)(2,1)} %all-gather.3.cloned.1.call-done.src_ref, bf16[8192,1,4096]{2,0,1:T(8,128)(2,1)} %param.7, s32[]{:T(128)S(6)} %select_n.159), kind=kOutput, calls=%fused_computation.41 | convolution fusion | flops 8590983168 | bytes 18874372 | tf_op jit(solution)/shard_map/dot_general | solution.py:51
  114.5 19.5 %collective-permute-done.3 = bf16[1024,1024]{1,0:T(8,128)(2,1)} collective-permute-done((bf16[1024,1024]{1,0:T(8,128)(2,1)}, bf16[1024,1024]{1,0:T(8,128)(2,1)}, u32[]{:S(2)}, u32[]{:S(2)}) %collective-permute-start.3) | collective-permute-done | bytes 2097184 | tf_op jit(solution)/shard_map/ppermute | solution.py:74
  134.0 15.3 %fusion.40 = (bf16[1024,1024]{1,0:T(8,128)(2,1)S(1)}, f32[1024,1024]{1,0:T(8,128)}) fusion(bf16[1024,1024]{1,0:T(8,128)(2,1)} %collective-permute-done.3, bf16[4096,1024]{1,0:T(8,128)(2,1)} %all-gather.3.cloned.1.call-done.src_ref, bf16[8192,1,4096]{2,0,1:T(8,128)(2,1)} %param.7, s32[]{:T(128)S(6)} %select_n.164), kind=kOutput, calls=%fused_computation.44 | convolution fusion | flops 8593080320 | bytes 25165828 | tf_op jit(solution)/shard_map/dot_general | solution.py:51
  156.2 12.4 %fusion.34 = bf16[1024,1024]{1,0:T(8,128)(2,1)} fusion(bf16[4096,1024]{1,0:T(8,128)(2,1)S(1)} %bitcast.126, bf16[8192,1,4096]{2,0,1:T(8,128)(2,1)} %param.7, s32[]{:T(128)S(6)} %select_n.161), kind=kOutput, calls=%fused_computation.42 | convolution fusion | flops 8590983168 | bytes 18874372 | tf_op jit(solution)/shard_map/dot_general | solution.py:51
  170.1 12.8 %fusion.10 = f32[1024,1024]{1,0:T(8,128)} fusion(bf16[4096,1024]{1,0:T(8,128)(2,1)S(1)} %bitcast.126, bf16[8192,1,4096]{2,0,1:T(8,128)(2,1)} %param.7, s32[]{:T(128)S(6)} %select_n.158), kind=kOutput, calls=%fused_computation.11 | convolution fusion | flops 8589934592 | bytes 20971524 | tf_op jit(solution)/shard_map/dot_general | solution.py:51
  182.9 13.6 %collective-permute-done.4 = bf16[1024,1024]{1,0:T(8,128)(2,1)} collective-permute-done((bf16[1024,1024]{1,0:T(8,128)(2,1)S(1)}, bf16[1024,1024]{1,0:T(8,128)(2,1)}, u32[]{:S(2)}, u32[]{:S(2)}) %collective-permute-start.4) | collective-permute-done | bytes 2097184 | tf_op jit(solution)/shard_map/ppermute | solution.py:82
  196.5 10.3 %add_convert_fusion.4 = (bf16[1024,1024]{1,0:T(8,128)(2,1)}, bf16[1024,1024]{1,0:T(8,128)(2,1)}) fusion(bf16[1024,1024]{1,0:T(8,128)(2,1)} %collective-permute-done.4, pred[]{:T(512)S(6)} %eq.45, f32[1024,1024]{1,0:T(8,128)} %get-tuple-element.21, bf16[1024,1024]{1,0:T(8,128)(2,1)} %collective-permute-done.3, f32[1024,1024]{1,0:T(8,128)} %fusion.10, ...), kind=kLoop, calls=%fused_computation.29 | loop fusion | flops 12582912 | bytes 20971522 | tf_op jit(solution)/shard_map/convert_element_type | solution.py:82
  206.8 5.8 collective-permute-start.5
  215.0 12.4 %fusion.28 = bf16[1024,1024]{1,0:T(8,128)(2,1)} fusion(bf16[4096,1024]{1,0:T(8,128)(2,1)S(1)} %bitcast.126, bf16[8192,1,4096]{2,0,1:T(8,128)(2,1)} %param.7, s32[]{:T(128)S(6)} %select_n.156), kind=kOutput, calls=%fused_computation.40 | convolution fusion | flops 8590983168 | bytes 18874372 | tf_op jit(solution)/shard_map/dot_general | solution.py:51
  233.4 12.8 %fusion.6 = f32[1024,1024]{1,0:T(8,128)S(1)} fusion(bf16[4096,1024]{1,0:T(8,128)(2,1)} %all-gather.3.cloned.1.call-done.src_ref, bf16[8192,1,4096]{2,0,1:T(8,128)(2,1)} %param.7, s32[]{:T(128)S(6)} %select_n.160), kind=kOutput, calls=%fused_computation.7 | convolution fusion | flops 8589934592 | bytes 20971524 | tf_op jit(solution)/shard_map/dot_general | solution.py:51
  246.2 8.3 %collective-permute-done.5 = bf16[1024,1024]{1,0:T(8,128)(2,1)} collective-permute-done((bf16[1024,1024]{1,0:T(8,128)(2,1)}, bf16[1024,1024]{1,0:T(8,128)(2,1)}, u32[]{:S(2)}, u32[]{:S(2)}) %collective-permute-start.5) | collective-permute-done | bytes 2097184 | tf_op jit(solution)/shard_map/ppermute | solution.py:82
  254.5 8.4 %add_convert_fusion.3 = (bf16[1024,1024]{1,0:T(8,128)(2,1)}, bf16[1024,1024]{1,0:T(8,128)(2,1)}) fusion(bf16[1024,1024]{1,0:T(8,128)(2,1)} %collective-permute-done.5, f32[1024,1024]{1,0:T(8,128)S(1)} %fusion.6, bf16[1024,1024]{1,0:T(8,128)(2,1)} %collective-permute-done.2, pred[]{:T(512)S(6)} %eq.44, f32[1024,1024]{1,0:T(8,128)S(1)} %copy-done.7, ...), kind=kLoop, calls=%fused_computation.28 | loop fusion | flops 12582912 | bytes 20971522 | tf_op jit(solution)/shard_map/convert_element_type | solution.py:82
  263.0 10.9 %collective-permute-start.6 = (bf16[1024,1024]{1,0:T(8,128)(2,1)}, bf16[1024,1024]{1,0:T(8,128)(2,1)}, u32[]{:S(2)}, u32[]{:S(2)}) collective-permute-start(bf16[1024,1024]{1,0:T(8,128)(2,1)} %get-tuple-element.9), channel_id=1, source_target_pairs={{0,2},{1,3},{2,4},{3,5},{4,6},{5,7},{8,10},{9,11},{10,12},{11,13},... | collective-permute-start | bytes 6291464 | tf_op jit(solution)/shard_map/ppermute | solution.py:82
  284.2 12.6 %fusion.14 = f32[1024,1024]{1,0:T(8,128)S(1)} fusion(bf16[4096,1024]{1,0:T(8,128)(2,1)} %all-gather.3.cloned.1.call-done.src_ref, bf16[8192,1,4096]{2,0,1:T(8,128)(2,1)} %param.7, s32[]{:T(128)S(6)} %select_n.155), kind=kOutput, calls=%fused_computation.15 | convolution fusion | flops 8589934592 | bytes 20971524 | tf_op jit(solution)/shard_map/dot_general | solution.py:51
  296.8 22.1 %collective-permute-done.6 = bf16[1024,1024]{1,0:T(8,128)(2,1)} collective-permute-done((bf16[1024,1024]{1,0:T(8,128)(2,1)}, bf16[1024,1024]{1,0:T(8,128)(2,1)}, u32[]{:S(2)}, u32[]{:S(2)}) %collective-permute-start.6) | collective-permute-done | bytes 2097184 | tf_op jit(solution)/shard_map/ppermute | solution.py:82
  318.9 9.6 %collective-permute-done.9 = bf16[1024,1024]{1,0:T(8,128)(2,1)} collective-permute-done((bf16[1024,1024]{1,0:T(8,128)(2,1)}, bf16[1024,1024]{1,0:T(8,128)(2,1)}, u32[]{:S(2)}, u32[]{:S(2)}) %collective-permute-start.9) | collective-permute-done | bytes 2097184 | tf_op jit(solution)/shard_map/ppermute | solution.py:82
  337.3 5.4 copy.46
  345.8 5.5 all-to-all-start.1
  353.6 49.3 %all-to-all-done.1 = bf16[8,8,128,128]{3,2,1,0:T(8,128)(2,1)} async-done(((bf16[8,8,128,128]{3,2,1,0:T(8,128)(2,1)}), bf16[8,8,128,128]{3,2,1,0:T(8,128)(2,1)}, u32[]{:S(2)}, u32[]{:S(2)}) %all-to-all-start.1) | async-done | bytes 2097184 | tf_op jit(solution)/shard_map/all_to_all | solution.py:55
  412.2 24.1 %all-to-all-done.3 = bf16[8,128,1024]{2,1,0:T(8,128)(2,1)S(1)} async-done(((bf16[8,128,1024]{2,1,0:T(8,128)(2,1)}), bf16[8,128,1024]{2,1,0:T(8,128)(2,1)S(1)}, u32[]{:S(2)}, u32[]{:S(2)}) %all-to-all-start.3) | async-done | bytes 2097184 | tf_op jit(solution)/shard_map/all_to_all | solution.py:55
  440.7 82.9 %reduce-scatter.4.cloned.1.call-done = f32[32,1024]{1,0:T(8,128)} async-done(((f32[1024,1024]{1,0:T(8,128)}), f32[32,1024]{1,0:T(8,128)}) %reduce-scatter.4.cloned.1.call-update) | async-done | bytes 131088 | tf_op jit(solution)/shard_map/reduce_scatter | solution.py:151
  545.9 57.3 %all-gather.5.cloned.1.call-done = bf16[1024,1024]{1,0:T(8,128)(2,1)} async-done(((bf16[32,1024]{1,0:T(8,128)(2,1)}), bf16[1024,1024]{1,0:T(8,128)(2,1)}) %all-gather.5.cloned.1.call-update) | async-done | bytes 2097168 | tf_op jit(solution)/shard_map/all_gather | solution.py:152
  (98 shorter events, 110.7 us)
Async XLA Ops:
  7.2 63.4 %all-gather.3.cloned.1.call-start = ((), (), s32[]{:S(2)}) async-start(), calls=%async_computation.8 | async-start | bytes 10485760 | tf_op jit(solution)/shard_map/all_gather | solution.py:136
  13.5 73.2 %copy-start.10 = (s32[8,4,8]{2,0,1:T(8,128)}, s32[8,4,8]{2,0,1:T(8,128)S(1)}, u32[]{:S(2)}) copy-start(s32[8,4,8]{2,0,1:T(8,128)S(1)} %get-tuple-element.8) | copy-start | bytes 3076
  13.5 73.4 %copy-start.3 = (bf16[1024,512]{1,0:T(8,128)(2,1)S(1)}, bf16[1024,512]{1,0:T(8,128)(2,1)}, u32[]{:S(2)}) copy-start(bf16[1024,512]{1,0:T(8,128)(2,1)} %src_ref.1) | copy-start | bytes 3145732
  85.2 48.8 %collective-permute-start.3 = (bf16[1024,1024]{1,0:T(8,128)(2,1)}, bf16[1024,1024]{1,0:T(8,128)(2,1)}, u32[]{:S(2)}, u32[]{:S(2)}) collective-permute-start(bf16[1024,1024]{1,0:T(8,128)(2,1)} %fusion.37), channel_id=1, source_target_pairs={{0,1},{1,0},{2,3},{3,2},{4,5},{5,4},{6,7},{7,6},{8,9},{9,8},{10,11... | collective-permute-start | bytes 6291464 | tf_op jit(solution)/shard_map/ppermute | solution.py:74
  90.0 139.0 %all-to-all-start.5 = ((bf16[8,128,512]{2,1,0:T(8,128)(2,1)}), bf16[8,128,512]{2,1,0:T(8,128)(2,1)S(1)}, u32[]{:S(2)}, u32[]{:S(2)}) async-start(bf16[8,128,512]{2,1,0:T(8,128)(2,1)} %shard_map.91), calls=%async_computation.5 | async-start | bytes 2097152 | tf_op jit(solution)/shard_map/all_to_all | solution.py:55
  95.7 60.5 %slice-start = ((s8[8388608]{0:T(1024)(128)(4,1)}), s8[4194304]{0:T(1024)(128)(4,1)S(1)}, s32[]{:S(2)}) async-start(s8[8388608]{0:T(1024)(128)(4,1)} %bitcast.125), calls=%async_computation.11 | async-start | bytes 8388608
  113.9 69.0 %collective-permute-start.1 = (bf16[1024,1024]{1,0:T(8,128)(2,1)S(1)}, bf16[1024,1024]{1,0:T(8,128)(2,1)}, u32[]{:S(2)}, u32[]{:S(2)}) collective-permute-start(bf16[1024,1024]{1,0:T(8,128)(2,1)S(1)} %fusion.31), channel_id=1, source_target_pairs={{0,1},{1,0},{2,3},{3,2},{4,5},{5,4},{6,7},{7,6},{8,9},{9,8},{10,11... | collective-permute-start | bytes 6291464 | tf_op jit(solution)/shard_map/ppermute | solution.py:74
  149.3 47.2 %collective-permute-start.4 = (bf16[1024,1024]{1,0:T(8,128)(2,1)S(1)}, bf16[1024,1024]{1,0:T(8,128)(2,1)}, u32[]{:S(2)}, u32[]{:S(2)}) collective-permute-start(bf16[1024,1024]{1,0:T(8,128)(2,1)S(1)} %get-tuple-element.20), channel_id=1, source_target_pairs={{0,2},{1,3},{8,10},{9,11},{16,18},{17,19},{24,26},{25,27}} | collective-permute-start | bytes 6291464 | tf_op jit(solution)/shard_map/ppermute | solution.py:82
  154.0 42.5 %collective-permute-start.7 = (bf16[1024,1024]{1,0:T(8,128)(2,1)S(1)}, bf16[1024,1024]{1,0:T(8,128)(2,1)}, u32[]{:S(2)}, u32[]{:S(2)}) collective-permute-start(bf16[1024,1024]{1,0:T(8,128)(2,1)S(1)} %get-tuple-element.20), channel_id=1, source_target_pairs={{6,4},{7,5},{14,12},{15,13},{22,20},{23,21},{30,28},{31,29}} | collective-permute-start | bytes 6291464 | tf_op jit(solution)/shard_map/ppermute | solution.py:82
  168.7 77.5 %collective-permute-start.2 = (bf16[1024,1024]{1,0:T(8,128)(2,1)}, bf16[1024,1024]{1,0:T(8,128)(2,1)}, u32[]{:S(2)}, u32[]{:S(2)}) collective-permute-start(bf16[1024,1024]{1,0:T(8,128)(2,1)} %fusion.34), channel_id=1, source_target_pairs={{0,1},{1,0},{2,3},{3,2},{4,5},{5,4},{6,7},{7,6},{8,9},{9,8},{10,11... | collective-permute-start | bytes 6291464 | tf_op jit(solution)/shard_map/ppermute | solution.py:74
  206.8 47.7 %collective-permute-start.5 = (bf16[1024,1024]{1,0:T(8,128)(2,1)}, bf16[1024,1024]{1,0:T(8,128)(2,1)}, u32[]{:S(2)}, u32[]{:S(2)}) collective-permute-start(bf16[1024,1024]{1,0:T(8,128)(2,1)} %get-tuple-element.11), channel_id=1, source_target_pairs={{0,2},{1,3},{2,4},{3,5},{8,10},{9,11},{10,12},{11,13},{16,18},{17,... | collective-permute-start | bytes 6291464 | tf_op jit(solution)/shard_map/ppermute | solution.py:82
  212.7 41.9 %collective-permute-start.8 = (bf16[1024,1024]{1,0:T(8,128)(2,1)}, bf16[1024,1024]{1,0:T(8,128)(2,1)}, u32[]{:S(2)}, u32[]{:S(2)}) collective-permute-start(bf16[1024,1024]{1,0:T(8,128)(2,1)} %get-tuple-element.12), channel_id=1, source_target_pairs={{4,2},{5,3},{6,4},{7,5},{12,10},{13,11},{14,12},{15,13},{20,18},{2... | collective-permute-start | bytes 6291464 | tf_op jit(solution)/shard_map/ppermute | solution.py:82
  227.5 69.3 %collective-permute-start = (bf16[1024,1024]{1,0:T(8,128)(2,1)}, bf16[1024,1024]{1,0:T(8,128)(2,1)}, u32[]{:S(2)}, u32[]{:S(2)}) collective-permute-start(bf16[1024,1024]{1,0:T(8,128)(2,1)} %fusion.28), channel_id=1, source_target_pairs={{0,1},{1,0},{2,3},{3,2},{4,5},{5,4},{6,7},{7,6},{8,9},{9,8},{10,11... | collective-permute-start | bytes 6291464 | tf_op jit(solution)/shard_map/ppermute | solution.py:74
  228.9 50.2 %all-to-all-start = ((bf16[4,8,2,128,128]{4,3,2,1,0:T(8,128)(2,1)}), bf16[4,8,2,128,128]{4,3,2,1,0:T(8,128)(2,1)}, u32[]{:S(2)}, u32[]{:S(2)}) async-start(bf16[4,8,2,128,128]{4,3,2,1,0:T(8,128)(2,1)} %bitcast.7), calls=%async_computation | async-start | bytes 4194304 | tf_op jit(solution)/shard_map/all_to_all | solution.py:55
  263.0 55.9 %collective-permute-start.6 = (bf16[1024,1024]{1,0:T(8,128)(2,1)}, bf16[1024,1024]{1,0:T(8,128)(2,1)}, u32[]{:S(2)}, u32[]{:S(2)}) collective-permute-start(bf16[1024,1024]{1,0:T(8,128)(2,1)} %get-tuple-element.9), channel_id=1, source_target_pairs={{0,2},{1,3},{2,4},{3,5},{4,6},{5,7},{8,10},{9,11},{10,12},{11,13},... | collective-permute-start | bytes 6291464 | tf_op jit(solution)/shard_map/ppermute | solution.py:82
  273.9 54.6 %collective-permute-start.9 = (bf16[1024,1024]{1,0:T(8,128)(2,1)}, bf16[1024,1024]{1,0:T(8,128)(2,1)}, u32[]{:S(2)}, u32[]{:S(2)}) collective-permute-start(bf16[1024,1024]{1,0:T(8,128)(2,1)} %get-tuple-element.10), channel_id=1, source_target_pairs={{2,0},{3,1},{4,2},{5,3},{6,4},{7,5},{10,8},{11,9},{12,10},{13,11},... | collective-permute-start | bytes 6291464 | tf_op jit(solution)/shard_map/ppermute | solution.py:82
  279.1 66.7 %all-to-all-start.6 = ((bf16[8,128,512]{2,1,0:T(8,128)(2,1)}), bf16[8,128,512]{2,1,0:T(8,128)(2,1)}, u32[]{:S(2)}, u32[]{:S(2)}) async-start(bf16[8,128,512]{2,1,0:T(8,128)(2,1)} %shard_map.92), calls=%async_computation.6 | async-start | bytes 2097152 | tf_op jit(solution)/shard_map/all_to_all | solution.py:55
  283.9 239.6 %reduce-scatter.4.cloned.1.call-start = ((), (), s32[]{:S(2)}) async-start(), calls=%async_computation.10 | async-start | bytes 4325376 | tf_op jit(solution)/shard_map/reduce_scatter | solution.py:151
  345.8 57.0 %all-to-all-start.1 = ((bf16[8,8,128,128]{3,2,1,0:T(8,128)(2,1)}), bf16[8,8,128,128]{3,2,1,0:T(8,128)(2,1)}, u32[]{:S(2)}, u32[]{:S(2)}) async-start(bf16[8,8,128,128]{3,2,1,0:T(8,128)(2,1)} %bitcast.129), calls=%async_computation.1 | async-start | bytes 4194304 | tf_op jit(solution)/shard_map/all_to_all | solution.py:55
  402.8 33.5 %all-to-all-start.3 = ((bf16[8,128,1024]{2,1,0:T(8,128)(2,1)}), bf16[8,128,1024]{2,1,0:T(8,128)(2,1)S(1)}, u32[]{:S(2)}, u32[]{:S(2)}) async-start(bf16[8,128,1024]{2,1,0:T(8,128)(2,1)} %copy-done), calls=%async_computation.3 | async-start | bytes 4194304 | tf_op jit(solution)/shard_map/all_to_all | solution.py:55
  436.3 91.1 %all-to-all-start.2 = ((bf16[8,128,1024]{2,1,0:T(8,128)(2,1)}), bf16[8,128,1024]{2,1,0:T(8,128)(2,1)}, u32[]{:S(2)}, u32[]{:S(2)}) async-start(bf16[8,128,1024]{2,1,0:T(8,128)(2,1)} %copy-done.2), calls=%async_computation.2 | async-start | bytes 4194304 | tf_op jit(solution)/shard_map/all_to_all | solution.py:55
  440.7 162.5 %all-gather.5.cloned.1.call-start = ((), (), s32[]{:S(2)}) async-start(), calls=%async_computation.9 | async-start | bytes 2162688 | tf_op jit(solution)/shard_map/all_gather | solution.py:152
  527.5 80.0 %all-to-all-start.4 = ((bf16[8,128,1024]{2,1,0:T(8,128)(2,1)}), bf16[8,128,1024]{2,1,0:T(8,128)(2,1)}, u32[]{:S(2)}, u32[]{:S(2)}) async-start(bf16[8,128,1024]{2,1,0:T(8,128)(2,1)} %shard_map.90), calls=%async_computation.4 | async-start | bytes 4194304 | tf_op jit(solution)/shard_map/all_to_all | solution.py:55
  545.9 61.5 %copy-start.9 = (bf16[512,1024]{1,0:T(8,128)(2,1)}, bf16[512,1024]{1,0:T(8,128)(2,1)S(1)}, u32[]{:S(2)}) copy-start(bf16[512,1024]{1,0:T(8,128)(2,1)S(1)} %bitcast_convert_fusion) | copy-start | bytes 3145732
  (9 other events, 145.5 us)
Sparse Core Ops, SparseCore 0:
  9.6 60.9 all-gather.2
  342.8 180.7 reduce-scatter.3
  526.6 76.5 all-gather.4

commit v2 on v1

--- a/solution.py
+++ b/solution.py
@@ -55,24 +55,28 @@
     return lax.all_to_all(x, axis, split_axis=0, concat_axis=0, tiled=True)
 
 
-def reduce_sets(panel_fock, gathered, dev_rows, num_sets, my_col):
+def reduce_sets(panel_fock, gathered, beside, dev_rows, num_sets, my_col):
     if num_sets != 8:
         part = dot32(panel_fock, gathered).astype(jnp.bfloat16)
-        return lax.psum_scatter(part, "col", scatter_dimension=0, tiled=True).astype(jnp.float32)
+        return lax.psum_scatter(part, "col", scatter_dimension=0, tiled=True), beside
     zi, xi = my_col // 2, my_col % 2
     order = jnp.array([[3, 2, 1, 0], [3, 2, 0, 1], [0, 1, 3, 2], [0, 1, 2, 3]], jnp.int32)
     mine = lax.dynamic_index_in_dim(order, zi, 0, keepdims=False)
     pairs = [(c, c ^ 1) for c in range(8)]
 
-    def part(dest_z, dest_x):
+    def part(dest_z, dest_x, gathered):
         rows = lax.dynamic_slice_in_dim(panel_fock, (dest_z * 2 + dest_x) * dev_rows, dev_rows, 0)
         return dot32(rows, gathered)
 
+    away = [part(mine[n], 1 - xi, gathered).astype(jnp.bfloat16) for n in range(4)]
+    came = [lax.ppermute(a, "col", pairs) for a in away]
+    gathered, _ = lax.optimization_barrier((gathered, away[3]))
     sums = []
     for n in range(4):
-        away = part(mine[n], 1 - xi).astype(jnp.bfloat16)
-        came = lax.ppermute(away, "col", pairs)
-        sums.append(part(mine[n], xi) + came.astype(jnp.float32))
+        if n == 3:
+            gathered, beside = lax.optimization_barrier((gathered, beside))
+        total = part(mine[n], xi, gathered) + came[n].astype(jnp.float32)
+        sums.append(total.astype(jnp.bfloat16))
 
     def hop(x, step, up):
         if up:
@@ -89,7 +93,7 @@
     down_own = jnp.where(zi == 2, sums[1], sums[2])
     up = hop(up_own + up, 2, True)
     down = hop(down_own + down, 2, False)
-    return sums[3] + up + down
+    return (sums[3] + up + down).astype(jnp.bfloat16), beside
 
 
 def body(fock, lmo_coef, three_index, rotation, lmo_ids, domains):
@@ -137,22 +141,33 @@
 
     tiles = pick(panel_fock, tile_rows, tile_cols, BLK)
     tiles = swap(tiles.reshape(num_panels, num_sets, per_panel, BLK, BLK), "row")
+    three_rows = swap(pick(three_index, row_pick), "row")
+    gathered, tiles, three_rows = lax.optimization_barrier((gathered, tiles, three_rows))
+    coef_dom = swap(pick(gathered, coef_pick), "col")
     tiles = jnp.transpose(tiles, (1, 0, 2, 3, 4)).reshape(num_sets, dom_blocks, BLK, BLK)
     tiles = swap(tiles, "col")
-
-    three_rows = swap(pick(three_index, row_pick), "row")
     three_dom = swap(pick(three_rows.reshape(dom_width, -1), set_pick), "col")
-    coef_dom = swap(pick(gathered, coef_pick), "col")
-
-    fock_coef = reduce_sets(panel_fock, gathered, dev_rows, num_sets, my_col)
-    coef_b = fock_coef.astype(jnp.bfloat16)
+
+    coef_b, (coef_dom, tiles, three_dom) = reduce_sets(
+        panel_fock, gathered, (coef_dom, tiles, three_dom), dev_rows, num_sets, my_col
+    )
 
     occ_term = jnp.einsum("ri,rj->ij", lmo_coef, coef_b, preferred_element_type=jnp.float32)
-    occ_part = lax.psum_scatter(occ_term, ("row", "col"), scatter_dimension=0, tiled=True)
-    occ_b = lax.all_gather(occ_part.astype(jnp.bfloat16), ("row", "col"), axis=0, tiled=True)
-
-    fc_rows = swap(pick(coef_b, row_pick), "row")
-    fc_dom = swap(pick(fc_rows.reshape(dom_width, -1), set_pick), "col")
+    occ_term = occ_term.astype(jnp.bfloat16).reshape(num_panels, -1, occ_term.shape[1])
+    fc_rows = pick(coef_b, row_pick).reshape(num_panels, per_panel * BLK, -1)
+    both = swap(jnp.concatenate([occ_term, fc_rows], axis=1), "row")
+    occ_rows = occ_term.shape[1]
+    occ_part = jnp.sum(both[:, :occ_rows].astype(jnp.float32), axis=0).astype(jnp.bfloat16)
+    fc_rows = both[:, occ_rows:].reshape(dom_width, -1)
+    occ_part = swap(occ_part.reshape(num_sets, -1, occ_part.shape[1]), "col")
+    occ_part = jnp.sum(occ_part.astype(jnp.float32), axis=0).astype(jnp.bfloat16)
+    fc_dom = swap(pick(fc_rows, set_pick), "col")
+    occ_part = swap(jnp.broadcast_to(occ_part, (num_sets, *occ_part.shape)), "col")
+    occ_part = occ_part.reshape(occ_rows, -1)
+    occ_pieces = [occ_part] + [
+        lax.ppermute(occ_part, "row", [(p, (p + step) % num_panels) for p in range(num_panels)])
+        for step in range(1, num_panels)
+    ]
 
     rot_set = pick(slot_rot, own_entry)
     rot_set = jnp.where(jnp.any(match, axis=1)[:, None, None], rot_set, jnp.zeros_like(rot_set))
@@ -168,7 +183,12 @@
     dom_fock = jnp.transpose(tiles, (1, 2, 0, 3)).reshape(dom_width, num_sets * BLK)
     fock_half = dot32(dom_fock, rot_set).astype(jnp.bfloat16)
     fock_rot = rotate(fock_half, rot_live)
-    proj_rot = (rotate(fc_dom, rot_set) - 0.5 * dot32(coef_rot, occ_b)).astype(jnp.bfloat16)
+    correction = 0.0
+    for step, piece in enumerate(occ_pieces):
+        start = (my_row - step) % num_panels * occ_rows
+        coef_cols = lax.dynamic_slice_in_dim(coef_rot, start, occ_rows, 1)
+        correction += dot32(coef_cols, piece)
+    proj_rot = (rotate(fc_dom, rot_set) - 0.5 * correction).astype(jnp.bfloat16)
     cross = jnp.einsum("mi,ni->mn", coef_rot, proj_rot, preferred_element_type=jnp.float32)
     proj_fock = fock_rot - cross - cross.T
     return (proj_fock[None, None], three_rot[None, None])

time: 633 us -> 623 us (0.984)
  waiting for transfers between devices: 344 us -> 249 us
  blocking collectives: 0 us -> 68.4 us
  starting transfers between devices: 63.4 us -> 87.5 us
  other arithmetic: 28.2 us -> 14.7 us
  matrix products: 130 us -> 139 us
    all_to_all x7, waiting for transfers between devices: 73.4 us -> 171 us  [swap(): return lax.all_to_all(x, axis, split_axis=0, concat_axis=0, tiled=True)]
    reduce_scatter x1 -> x0, waiting for transfers between devices: 82.9 us -> none  [body(): lax.psum_scatter(occ_term, ('row', 'col'), scatter_dimension=0, tiled=True)]
    all_to_all x0 -> x2, blocking collectives: none -> 68.4 us  [swap(): return lax.all_to_all(x, axis, split_axis=0, concat_axis=0, tiled=True)]
    all_gather x1 -> x0, waiting for transfers between devices: 57.3 us -> none  [body(): lax.all_gather(occ_part.astype(jnp.bfloat16), ('row', 'col'), axis=0, til...]
    all_gather x1, waiting for transfers between devices: 57.1 us -> 7.52 us  [body(): gathered = lax.all_gather(lmo_coef, 'row', axis=0, tiled=True)]
    ppermute x6, starting transfers between devices: 27.3 us -> 43.6 us  [hop(): return lax.ppermute(x.astype(jnp.bfloat16), 'col', perm).astype(jnp.float32)]
    ppermute x6, waiting for transfers between devices: 53.6 us -> 42 us  [hop(): return lax.ppermute(x.astype(jnp.bfloat16), 'col', perm).astype(jnp.float32)]
    convert_element_type x2, other arithmetic: 18.8 us -> 7.59 us  [hop(): return lax.ppermute(x.astype(jnp.bfloat16), 'col', perm).astype(jnp.float32)]
  transfers between devices with their start and end apart: 20 -> 21, of which waited for: 10 -> 13; matrix products, arithmetic and copies ran while one was open for 24% -> 22% of each run, Pallas kernels for 3% -> 3%
where the time goes in v2:
time: 623 us; the launch traced here: 614 us
  waiting for transfers between devices  249 us (40%)
  matrix products  139 us (22%)
  starting transfers between devices  87.5 us (14%)
  blocking collectives  68.4 us (11%)
  local copies, waits for them, and re-layouts  19.9 us (3%)
  Pallas kernels  18.1 us (3%)
  between operations  17.5 us (3%)
  other arithmetic  14.7 us (2%)
    all_to_all x7, waiting for transfers between devices, swap(): return lax.all_to_all(x, axis, split_axis=0, concat_axis=0, tiled=True)  171 us
    dot_general x11, matrix products, dot32(): return jnp.dot(a, b, preferred_element_type=jnp.float32)  117 us
    all_to_all x2, blocking collectives, swap(): return lax.all_to_all(x, axis, split_axis=0, concat_axis=0, tiled=True)  68.4 us
    ppermute x6, starting transfers between devices, hop(): return lax.ppermute(x.astype(jnp.bfloat16), 'col', perm).astype(jnp.float32)  43.6 us
    ppermute x6, waiting for transfers between devices, hop(): return lax.ppermute(x.astype(jnp.bfloat16), 'col', perm).astype(jnp.float32)  42 us
    all_to_all x7, starting transfers between devices, swap(): return lax.all_to_all(x, axis, split_axis=0, concat_axis=0, tiled=True)  34.9 us
    ppermute x4, waiting for transfers between devices, reduce_sets(): came = [lax.ppermute(a, 'col', pairs) for a in away]  19.7 us
    pallas_call x7, Pallas kernels, pick(): pl.pallas_call(functools.partial(pick_kernel, count, width), out_shape=ja...  18.1 us
  transfers between devices with their start and end apart: 21, of which 13 were waited for; matrix products, arithmetic and copies ran while one was open for 22% of the time, Pallas kernels for 3%

profile of v2, /device:TPU:0, one launch (start us, length us, event | category | flops | bytes accessed | tf_op | source)
XLA Modules:
  0.0 613.5 jit_solution(14220841607414479977)
XLA Ops:
  22.3 18.4 %all-to-all-done.1 = bf16[8,128,512]{2,1,0:T(8,128)(2,1)S(1)} async-done(((bf16[8,128,512]{2,1,0:T(8,128)(2,1)}), bf16[8,128,512]{2,1,0:T(8,128)(2,1)S(1)}, u32[]{:S(2)}, u32[]{:S(2)}) %all-to-all-start.1) | async-done | bytes 1048608 | tf_op jit(solution)/shard_map/all_to_all | solution.py:55
  49.4 44.3 %all-to-all-done = bf16[4,8,2,128,128]{4,3,2,1,0:T(8,128)(2,1)} async-done(((bf16[4,8,2,128,128]{4,3,2,1,0:T(8,128)(2,1)}), bf16[4,8,2,128,128]{4,3,2,1,0:T(8,128)(2,1)}, u32[]{:S(2)}, u32[]{:S(2)}) %all-to-all-start) | async-done | bytes 2097184 | tf_op jit(solution)/shard_map/all_to_all | solution.py:55
  93.7 7.5 %all-gather.2.cloned.1.call-done.src_ref = bf16[4096,1024]{1,0:T(8,128)(2,1)} async-done(((bf16[1024,1024]{1,0:T(8,128)(2,1)}), bf16[4096,1024]{1,0:T(8,128)(2,1)}) %all-gather.2.cloned.1.call-update) | async-done | bytes 8388624 | tf_op jit(solution)/shard_map/all_gather | solution.py:140
  101.2 14.5 %fusion.37 = bf16[1024,1024]{1,0:T(8,128)(2,1)S(1)} fusion(bf16[4096,1024]{1,0:T(8,128)(2,1)} %all-gather.2.cloned.1.call-done.src_ref, bf16[8192,1,4096]{2,0,1:T(8,128)(2,1)} %param.7, s32[]{:T(128)S(6)} %select_n.193), kind=kOutput, calls=%fused_computation.45 | convolution fusion | flops 8590983168 | bytes 18874372 | tf_op jit(solution)/shard_map/dot_general | solution.py:51
  118.0 12.3 %fusion.28 = bf16[1024,1024]{1,0:T(8,128)(2,1)} fusion(bf16[4096,1024]{1,0:T(8,128)(2,1)S(1)} %copy-done, bf16[8192,1,4096]{2,0,1:T(8,128)(2,1)} %param.7, s32[]{:T(128)S(6)} %select_n.179), kind=kOutput, calls=%fused_computation.42 | convolution fusion | flops 8590983168 | bytes 18874372 | tf_op jit(solution)/shard_map/dot_general | solution.py:51
  138.4 14.6 %fusion.31 = bf16[1024,1024]{1,0:T(8,128)(2,1)} fusion(bf16[4096,1024]{1,0:T(8,128)(2,1)} %all-gather.2.cloned.1.call-done.src_ref, bf16[8192,1,4096]{2,0,1:T(8,128)(2,1)} %param.7, s32[]{:T(128)S(6)} %select_n.187), kind=kOutput, calls=%fused_computation.43 | convolution fusion | flops 8590983168 | bytes 18874372 | tf_op jit(solution)/shard_map/dot_general | solution.py:51
  160.6 15.0 %all-to-all-done.4 = bf16[8,128,512]{2,1,0:T(8,128)(2,1)S(1)} async-done(((bf16[8,128,512]{2,1,0:T(8,128)(2,1)}), bf16[8,128,512]{2,1,0:T(8,128)(2,1)S(1)}, u32[]{:S(2)}, u32[]{:S(2)}) %all-to-all-start.4) | async-done | bytes 1048608 | tf_op jit(solution)/shard_map/all_to_all | solution.py:55
  176.6 6.4 %all-to-all-start.2 = ((bf16[8,128,1024]{2,1,0:T(8,128)(2,1)}), bf16[8,128,1024]{2,1,0:T(8,128)(2,1)}, u32[]{:S(2)}, u32[]{:S(2)}) async-start(bf16[8,128,1024]{2,1,0:T(8,128)(2,1)} %shard_map.88), calls=%async_computation.2 | async-start | bytes 4194304 | tf_op jit(solution)/shard_map/all_to_all | solution.py:55
  183.0 14.7 %fusion.34 = bf16[1024,1024]{1,0:T(8,128)(2,1)} fusion(bf16[4096,1024]{1,0:T(8,128)(2,1)} %all-gather.2.cloned.1.call-done.src_ref, bf16[8192,1,4096]{2,0,1:T(8,128)(2,1)} %param.7, s32[]{:T(128)S(6)} %select_n.189), kind=kOutput, calls=%fused_computation.44 | convolution fusion | flops 8590983168 | bytes 18874372 | tf_op jit(solution)/shard_map/dot_general | solution.py:51
  202.9 14.0 %add_convert_fusion.5 = bf16[1024,1024]{1,0:T(8,128)(2,1)S(1)} fusion(bf16[1024,1024]{1,0:T(8,128)(2,1)} %collective-permute-done.3, bf16[4096,1024]{1,0:T(8,128)(2,1)} %all-gather.2.cloned.1.call-done.src_ref, bf16[8192,1,4096]{2,0,1:T(8,128)(2,1)} %param.7, s32[]{:T(128)S(6)} %select_n.192), kind=kOutput, calls=%fused_computation.31 | convolution fusion | flops 8593080320 | bytes 20971524 | tf_op jit(solution)/shard_map/dot_general | solution.py:51
  223.7 64.5 %all-to-all-done.2 = bf16[8,128,1024]{2,1,0:T(8,128)(2,1)} async-done(((bf16[8,128,1024]{2,1,0:T(8,128)(2,1)}), bf16[8,128,1024]{2,1,0:T(8,128)(2,1)}, u32[]{:S(2)}, u32[]{:S(2)}) %all-to-all-start.2) | async-done | bytes 2097184 | tf_op jit(solution)/shard_map/all_to_all | solution.py:55
  288.1 6.4 %all-to-all-start.3 = ((bf16[8,8,128,128]{3,2,1,0:T(8,128)(2,1)}), bf16[8,8,128,128]{3,2,1,0:T(8,128)(2,1)}, u32[]{:S(2)}, u32[]{:S(2)}) async-start(bf16[8,8,128,128]{3,2,1,0:T(8,128)(2,1)} %bitcast.13), calls=%async_computation.3 | async-start | bytes 4194304 | tf_op jit(solution)/shard_map/all_to_all | solution.py:55
  294.5 14.0 %add_convert_fusion.7 = bf16[1024,1024]{1,0:T(8,128)(2,1)S(1)} fusion(bf16[1024,1024]{1,0:T(8,128)(2,1)} %collective-permute-done.1, bf16[4096,1024]{1,0:T(8,128)(2,1)} %all-gather.2.cloned.1.call-done.src_ref, bf16[8192,1,4096]{2,0,1:T(8,128)(2,1)} %param.7, s32[]{:T(128)S(6)} %select_n.186), kind=kOutput, calls=%fused_computation.33 | convolution fusion | flops 8593080320 | bytes 20971524 | tf_op jit(solution)/shard_map/dot_general | solution.py:51
  312.5 16.8 %collective-permute-start.5 = (bf16[1024,1024]{1,0:T(8,128)(2,1)S(1)}, bf16[1024,1024]{1,0:T(8,128)(2,1)S(1)}, u32[]{:S(2)}, u32[]{:S(2)}) collective-permute-start(bf16[1024,1024]{1,0:T(8,128)(2,1)S(1)} %get-tuple-element.29), channel_id=1, source_target_pairs={{0,2},{1,3},{2,4},{3,5},{8,10},{9,11},{10,12},{11,13},{16,18},{17,... | collective-permute-start | bytes 6291464 | tf_op jit(solution)/shard_map/ppermute | solution.py:86
  330.2 19.7 %collective-permute-done.2 = bf16[1024,1024]{1,0:T(8,128)(2,1)} collective-permute-done((bf16[1024,1024]{1,0:T(8,128)(2,1)}, bf16[1024,1024]{1,0:T(8,128)(2,1)}, u32[]{:S(2)}, u32[]{:S(2)}) %collective-permute-start.2) | collective-permute-done | bytes 2097184 | tf_op jit(solution)/shard_map/ppermute | solution.py:72
  349.9 14.0 %add_convert_fusion.6 = bf16[1024,1024]{1,0:T(8,128)(2,1)S(1)} fusion(bf16[1024,1024]{1,0:T(8,128)(2,1)} %collective-permute-done.2, bf16[4096,1024]{1,0:T(8,128)(2,1)} %all-gather.2.cloned.1.call-done.src_ref, bf16[8192,1,4096]{2,0,1:T(8,128)(2,1)} %param.7, s32[]{:T(128)S(6)} %select_n.188), kind=kOutput, calls=%fused_computation.32 | convolution fusion | flops 8593080320 | bytes 20971524 | tf_op jit(solution)/shard_map/dot_general | solution.py:51
  363.9 8.6 %collective-permute-done.5 = bf16[1024,1024]{1,0:T(8,128)(2,1)S(1)} collective-permute-done((bf16[1024,1024]{1,0:T(8,128)(2,1)S(1)}, bf16[1024,1024]{1,0:T(8,128)(2,1)S(1)}, u32[]{:S(2)}, u32[]{:S(2)}) %collective-permute-start.5) | collective-permute-done | bytes 2097184 | tf_op jit(solution)/shard_map/ppermute | solution.py:86
  376.1 18.0 %collective-permute-start.6 = (bf16[1024,1024]{1,0:T(8,128)(2,1)}, bf16[1024,1024]{1,0:T(8,128)(2,1)}, u32[]{:S(2)}, u32[]{:S(2)}) collective-permute-start(bf16[1024,1024]{1,0:T(8,128)(2,1)} %get-tuple-element.27), channel_id=1, source_target_pairs={{0,2},{1,3},{2,4},{3,5},{4,6},{5,7},{8,10},{9,11},{10,12},{11,13},... | collective-permute-start | bytes 6291464 | tf_op jit(solution)/shard_map/ppermute | solution.py:86
  395.4 12.6 %fusion.12 = f32[1024,1024]{1,0:T(8,128)S(1)} fusion(bf16[4096,1024]{1,0:T(8,128)(2,1)} %all-gather.2.cloned.1.call-done.src_ref, bf16[8192,1,4096]{2,0,1:T(8,128)(2,1)} %param.7, s32[]{:T(128)S(6)} %select_n.184), kind=kOutput, calls=%fused_computation.13 | convolution fusion | flops 8589934592 | bytes 20971524 | tf_op jit(solution)/shard_map/dot_general | solution.py:51
  408.1 28.1 %collective-permute-done.6 = bf16[1024,1024]{1,0:T(8,128)(2,1)} collective-permute-done((bf16[1024,1024]{1,0:T(8,128)(2,1)}, bf16[1024,1024]{1,0:T(8,128)(2,1)}, u32[]{:S(2)}, u32[]{:S(2)}) %collective-permute-start.6) | collective-permute-done | bytes 2097184 | tf_op jit(solution)/shard_map/ppermute | solution.py:86
  449.9 50.7 %all_to_all.45 = bf16[4,512,1024]{2,1,0:T(8,128)(2,1)S(1)} all-to-all(bf16[4,512,1024]{2,1,0:T(8,128)(2,1)S(1)} %pad_maximum_fusion), channel_id=1, replica_groups=mesh['row'=4,'col'=8] {'row'}, dimensions={0} | all-to-all | bytes 8388608 | tf_op jit(solution)/shard_map/all_to_all | solution.py:55
  501.3 17.6 %all_to_all.46 = bf16[8,32,1024]{2,1,0:T(8,128)(2,1)S(1)} all-to-all(bf16[8,32,1024]{2,1,0:T(8,128)(2,1)S(1)} %bitcast.141), channel_id=1, replica_groups=mesh['row'=4,'col'=8] {'col'}, dimensions={0} | all-to-all | bytes 1048576 | tf_op jit(solution)/shard_map/all_to_all | solution.py:55
  526.3 11.4 %all-to-all-done.8 = bf16[8,32,1024]{2,1,0:T(8,128)(2,1)} async-done(((bf16[8,32,1024]{2,1,0:T(8,128)(2,1)}), bf16[8,32,1024]{2,1,0:T(8,128)(2,1)}, u32[]{:S(2)}, u32[]{:S(2)}) %all-to-all-start.8) | async-done | bytes 524320 | tf_op jit(solution)/shard_map/all_to_all | solution.py:55
  572.0 17.0 %all-to-all-done.6 = bf16[8,128,1024]{2,1,0:T(8,128)(2,1)} async-done(((bf16[8,128,1024]{2,1,0:T(8,128)(2,1)}), bf16[8,128,1024]{2,1,0:T(8,128)(2,1)}, u32[]{:S(2)}, u32[]{:S(2)}) %all-to-all-start.6) | async-done | bytes 2097184 | tf_op jit(solution)/shard_map/all_to_all | solution.py:55
  (104 shorter events, 134.7 us)
Async XLA Ops:
  7.2 94.0 %all-gather.2.cloned.1.call-start = ((), (), s32[]{:S(2)}) async-start(), calls=%async_computation.9 | async-start | bytes 10485760 | tf_op jit(solution)/shard_map/all_gather | solution.py:140
  13.3 27.4 %all-to-all-start.1 = ((bf16[8,128,512]{2,1,0:T(8,128)(2,1)}), bf16[8,128,512]{2,1,0:T(8,128)(2,1)S(1)}, u32[]{:S(2)}, u32[]{:S(2)}) async-start(bf16[8,128,512]{2,1,0:T(8,128)(2,1)} %shard_map.87), calls=%async_computation.1 | async-start | bytes 2097152 | tf_op jit(solution)/shard_map/all_to_all | solution.py:55
  40.7 53.0 %all-to-all-start = ((bf16[4,8,2,128,128]{4,3,2,1,0:T(8,128)(2,1)}), bf16[4,8,2,128,128]{4,3,2,1,0:T(8,128)(2,1)}, u32[]{:S(2)}, u32[]{:S(2)}) async-start(bf16[4,8,2,128,128]{4,3,2,1,0:T(8,128)(2,1)} %bitcast.7), calls=%async_computation | async-start | bytes 4194304 | tf_op jit(solution)/shard_map/all_to_all | solution.py:55
  49.4 81.0 %copy-start.4 = (s32[8]{0:T(128)}, s32[8]{0:T(128)S(1)}, u32[]{:S(2)}) copy-start(s32[8]{0:T(128)S(1)} %get-tuple-element.18.row_ref) | copy-start | bytes 100
  115.7 87.2 %collective-permute-start.3 = (bf16[1024,1024]{1,0:T(8,128)(2,1)S(1)}, bf16[1024,1024]{1,0:T(8,128)(2,1)}, u32[]{:S(2)}, u32[]{:S(2)}) collective-permute-start(bf16[1024,1024]{1,0:T(8,128)(2,1)S(1)} %fusion.37), channel_id=1, source_target_pairs={{0,1},{1,0},{2,3},{3,2},{4,5},{5,4},{6,7},{7,6},{8,9},{9,8},{10,11... | collective-permute-start | bytes 6291464 | tf_op jit(solution)/shard_map/ppermute | solution.py:72
  133.4 42.2 %all-to-all-start.4 = ((bf16[8,128,512]{2,1,0:T(8,128)(2,1)}), bf16[8,128,512]{2,1,0:T(8,128)(2,1)S(1)}, u32[]{:S(2)}, u32[]{:S(2)}) async-start(bf16[8,128,512]{2,1,0:T(8,128)(2,1)} %shard_map.89), calls=%async_computation.4 | async-start | bytes 2097152 | tf_op jit(solution)/shard_map/all_to_all | solution.py:55
  153.0 255.1 %collective-permute-start = (bf16[1024,1024]{1,0:T(8,128)(2,1)}, bf16[1024,1024]{1,0:T(8,128)(2,1)}, u32[]{:S(2)}, u32[]{:S(2)}) collective-permute-start(bf16[1024,1024]{1,0:T(8,128)(2,1)} %fusion.28), channel_id=1, source_target_pairs={{0,1},{1,0},{2,3},{3,2},{4,5},{5,4},{6,7},{7,6},{8,9},{9,8},{10,11... | collective-permute-start | bytes 6291464 | tf_op jit(solution)/shard_map/ppermute | solution.py:72
  155.0 139.5 %collective-permute-start.1 = (bf16[1024,1024]{1,0:T(8,128)(2,1)}, bf16[1024,1024]{1,0:T(8,128)(2,1)}, u32[]{:S(2)}, u32[]{:S(2)}) collective-permute-start(bf16[1024,1024]{1,0:T(8,128)(2,1)} %fusion.31), channel_id=1, source_target_pairs={{0,1},{1,0},{2,3},{3,2},{4,5},{5,4},{6,7},{7,6},{8,9},{9,8},{10,11... | collective-permute-start | bytes 6291464 | tf_op jit(solution)/shard_map/ppermute | solution.py:72
  176.6 111.5 %all-to-all-start.2 = ((bf16[8,128,1024]{2,1,0:T(8,128)(2,1)}), bf16[8,128,1024]{2,1,0:T(8,128)(2,1)}, u32[]{:S(2)}, u32[]{:S(2)}) async-start(bf16[8,128,1024]{2,1,0:T(8,128)(2,1)} %shard_map.88), calls=%async_computation.2 | async-start | bytes 4194304 | tf_op jit(solution)/shard_map/all_to_all | solution.py:55
  197.8 152.1 %collective-permute-start.2 = (bf16[1024,1024]{1,0:T(8,128)(2,1)}, bf16[1024,1024]{1,0:T(8,128)(2,1)}, u32[]{:S(2)}, u32[]{:S(2)}) collective-permute-start(bf16[1024,1024]{1,0:T(8,128)(2,1)} %fusion.34), channel_id=1, source_target_pairs={{0,1},{1,0},{2,3},{3,2},{4,5},{5,4},{6,7},{7,6},{8,9},{9,8},{10,11... | collective-permute-start | bytes 6291464 | tf_op jit(solution)/shard_map/ppermute | solution.py:72
  216.9 91.6 %collective-permute-start.4 = (bf16[1024,1024]{1,0:T(8,128)(2,1)S(1)}, bf16[1024,1024]{1,0:T(8,128)(2,1)}, u32[]{:S(2)}, u32[]{:S(2)}) collective-permute-start(bf16[1024,1024]{1,0:T(8,128)(2,1)S(1)} %add_convert_fusion.5), channel_id=1, source_target_pairs={{0,2},{1,3},{8,10},{9,11},{16,18},{17,19},{24,26},{25,27}} | collective-permute-start | bytes 6291464 | tf_op jit(solution)/shard_map/ppermute | solution.py:86
  221.7 86.9 %collective-permute-start.7 = (bf16[1024,1024]{1,0:T(8,128)(2,1)S(1)}, bf16[1024,1024]{1,0:T(8,128)(2,1)}, u32[]{:S(2)}, u32[]{:S(2)}) collective-permute-start(bf16[1024,1024]{1,0:T(8,128)(2,1)S(1)} %add_convert_fusion.5), channel_id=1, source_target_pairs={{6,4},{7,5},{14,12},{15,13},{22,20},{23,21},{30,28},{31,29}} | collective-permute-start | bytes 6291464 | tf_op jit(solution)/shard_map/ppermute | solution.py:86
  288.1 107.3 %all-to-all-start.3 = ((bf16[8,8,128,128]{3,2,1,0:T(8,128)(2,1)}), bf16[8,8,128,128]{3,2,1,0:T(8,128)(2,1)}, u32[]{:S(2)}, u32[]{:S(2)}) async-start(bf16[8,8,128,128]{3,2,1,0:T(8,128)(2,1)} %bitcast.13), calls=%async_computation.3 | async-start | bytes 4194304 | tf_op jit(solution)/shard_map/all_to_all | solution.py:55
  312.5 60.0 %collective-permute-start.5 = (bf16[1024,1024]{1,0:T(8,128)(2,1)S(1)}, bf16[1024,1024]{1,0:T(8,128)(2,1)S(1)}, u32[]{:S(2)}, u32[]{:S(2)}) collective-permute-start(bf16[1024,1024]{1,0:T(8,128)(2,1)S(1)} %get-tuple-element.29), channel_id=1, source_target_pairs={{0,2},{1,3},{2,4},{3,5},{8,10},{9,11},{10,12},{11,13},{16,18},{17,... | collective-permute-start | bytes 6291464 | tf_op jit(solution)/shard_map/ppermute | solution.py:86
  329.4 43.1 %collective-permute-start.8 = (bf16[1024,1024]{1,0:T(8,128)(2,1)S(1)}, bf16[1024,1024]{1,0:T(8,128)(2,1)S(1)}, u32[]{:S(2)}, u32[]{:S(2)}) collective-permute-start(bf16[1024,1024]{1,0:T(8,128)(2,1)S(1)} %get-tuple-element.30), channel_id=1, source_target_pairs={{4,2},{5,3},{6,4},{7,5},{12,10},{13,11},{14,12},{15,13},{20,18},{2... | collective-permute-start | bytes 6291464 | tf_op jit(solution)/shard_map/ppermute | solution.py:86
  376.1 60.1 %collective-permute-start.6 = (bf16[1024,1024]{1,0:T(8,128)(2,1)}, bf16[1024,1024]{1,0:T(8,128)(2,1)}, u32[]{:S(2)}, u32[]{:S(2)}) collective-permute-start(bf16[1024,1024]{1,0:T(8,128)(2,1)} %get-tuple-element.27), channel_id=1, source_target_pairs={{0,2},{1,3},{2,4},{3,5},{4,6},{5,7},{8,10},{9,11},{10,12},{11,13},... | collective-permute-start | bytes 6291464 | tf_op jit(solution)/shard_map/ppermute | solution.py:86
  394.1 47.4 %collective-permute-start.9 = (bf16[1024,1024]{1,0:T(8,128)(2,1)S(1)}, bf16[1024,1024]{1,0:T(8,128)(2,1)}, u32[]{:S(2)}, u32[]{:S(2)}) collective-permute-start(bf16[1024,1024]{1,0:T(8,128)(2,1)S(1)} %get-tuple-element.28), channel_id=1, source_target_pairs={{2,0},{3,1},{4,2},{5,3},{6,4},{7,5},{10,8},{11,9},{12,10},{13,11},... | collective-permute-start | bytes 6291464 | tf_op jit(solution)/shard_map/ppermute | solution.py:86
  408.0 38.1 %copy-start.7 = (bf16[1024,1024]{1,0:T(8,128)(2,1)S(1)}, bf16[1024,1024]{1,0:T(8,128)(2,1)}, u32[]{:S(2)}) copy-start(bf16[1024,1024]{1,0:T(8,128)(2,1)} %param.8) | copy-start | bytes 6291460
  501.3 22.7 %copy-start.5 = (s32[8]{0:T(128)S(1)}, s32[8]{0:T(128)}, u32[]{:S(2)}) copy-start(s32[8]{0:T(128)} %copy-done.4) | copy-start | bytes 100
  519.9 17.8 %all-to-all-start.8 = ((bf16[8,32,1024]{2,1,0:T(8,128)(2,1)}), bf16[8,32,1024]{2,1,0:T(8,128)(2,1)}, u32[]{:S(2)}, u32[]{:S(2)}) async-start(bf16[8,32,1024]{2,1,0:T(8,128)(2,1)} %broadcast_in_dim.90), calls=%async_computation.8 | async-start | bytes 1048576 | tf_op jit(solution)/shard_map/all_to_all | solution.py:55
  537.7 51.4 %all-to-all-start.6 = ((bf16[8,128,1024]{2,1,0:T(8,128)(2,1)}), bf16[8,128,1024]{2,1,0:T(8,128)(2,1)}, u32[]{:S(2)}, u32[]{:S(2)}) async-start(bf16[8,128,1024]{2,1,0:T(8,128)(2,1)} %shard_map.92), calls=%async_computation.6 | async-start | bytes 4194304 | tf_op jit(solution)/shard_map/all_to_all | solution.py:55
  553.3 12.5 %collective-permute-start.10 = (bf16[256,1024]{1,0:T(8,128)(2,1)}, bf16[256,1024]{1,0:T(8,128)(2,1)S(1)}, u32[]{:S(2)}, u32[]{:S(2)}) collective-permute-start(bf16[256,1024]{1,0:T(8,128)(2,1)} %bitcast.35), channel_id=1, source_target_pairs={{0,8},{8,16},{16,24},{24,0},{1,9},{9,17},{17,25},{25,1},{2,10},{10... | collective-permute-start | bytes 1572872 | tf_op jit(solution)/shard_map/ppermute | solution.py:168
  555.2 15.1 %collective-permute-start.11 = (bf16[256,1024]{1,0:T(8,128)(2,1)}, bf16[256,1024]{1,0:T(8,128)(2,1)S(1)}, u32[]{:S(2)}, u32[]{:S(2)}) collective-permute-start(bf16[256,1024]{1,0:T(8,128)(2,1)} %bitcast.35), channel_id=1, source_target_pairs={{0,16},{8,24},{16,0},{24,8},{1,17},{9,25},{17,1},{25,9},{2,18},{10... | collective-permute-start | bytes 1572872 | tf_op jit(solution)/shard_map/ppermute | solution.py:168
  556.0 37.2 %collective-permute-start.12 = (bf16[256,1024]{1,0:T(8,128)(2,1)}, bf16[256,1024]{1,0:T(8,128)(2,1)}, u32[]{:S(2)}, u32[]{:S(2)}) collective-permute-start(bf16[256,1024]{1,0:T(8,128)(2,1)} %bitcast.35), channel_id=1, source_target_pairs={{0,24},{8,0},{16,8},{24,16},{1,25},{9,1},{17,9},{25,17},{2,26},{10... | collective-permute-start | bytes 1572872 | tf_op jit(solution)/shard_map/ppermute | solution.py:168
  (10 other events, 49.7 us)
Sparse Core Ops, SparseCore 0:
  9.6 91.5 all-gather.1

commit v3 on v2

--- a/solution.py
+++ b/solution.py
@@ -73,8 +73,6 @@
     gathered, _ = lax.optimization_barrier((gathered, away[3]))
     sums = []
     for n in range(4):
-        if n == 3:
-            gathered, beside = lax.optimization_barrier((gathered, beside))
         total = part(mine[n], xi, gathered) + came[n].astype(jnp.float32)
         sums.append(total.astype(jnp.bfloat16))
 
@@ -142,7 +140,6 @@
     tiles = pick(panel_fock, tile_rows, tile_cols, BLK)
     tiles = swap(tiles.reshape(num_panels, num_sets, per_panel, BLK, BLK), "row")
     three_rows = swap(pick(three_index, row_pick), "row")
-    gathered, tiles, three_rows = lax.optimization_barrier((gathered, tiles, three_rows))
     coef_dom = swap(pick(gathered, coef_pick), "col")
     tiles = jnp.transpose(tiles, (1, 0, 2, 3, 4)).reshape(num_sets, dom_blocks, BLK, BLK)
     tiles = swap(tiles, "col")

time: 623 us -> 662 us (1.063)
  waiting for transfers between devices: 249 us -> 377 us
  blocking collectives: 68.4 us -> 0 us
  starting transfers between devices: 87.5 us -> 67.6 us
  matrix products: 139 us -> 129 us
  other arithmetic: 14.7 us -> 22.7 us
    ppermute x4, waiting for transfers between devices: 19.7 us -> 99.1 us  [reduce_sets(): came = [lax.ppermute(a, 'col', pairs) for a in away]]
    all_to_all x2 -> x0, blocking collectives: 68.4 us -> none  [swap(): return lax.all_to_all(x, axis, split_axis=0, concat_axis=0, tiled=True)]
    all_gather x1, waiting for transfers between devices: 7.52 us -> 52.5 us  [body(): gathered = lax.all_gather(lmo_coef, 'row', axis=0, tiled=True)]
    ppermute x6, starting transfers between devices: 43.6 us -> 21.5 us  [hop(): return lax.ppermute(x.astype(jnp.bfloat16), 'col', perm).astype(jnp.float32)]
    dot_general x11, matrix products: 117 us -> 106 us  [dot32(): return jnp.dot(a, b, preferred_element_type=jnp.float32)]
    all_to_all x7 -> x9, waiting for transfers between devices: 171 us -> 179 us  [swap(): return lax.all_to_all(x, axis, split_axis=0, concat_axis=0, tiled=True)]
    all_to_all x7 -> x9, starting transfers between devices: 34.9 us -> 39.5 us  [swap(): return lax.all_to_all(x, axis, split_axis=0, concat_axis=0, tiled=True)]
  transfers between devices with their start and end apart: 21 -> 23, of which waited for: 13 -> 16; matrix products, arithmetic and copies ran while one was open for 22% -> 23% of each run, Pallas kernels for 3% -> 3%
where the time goes in v3:
time: 662 us; the launch traced here: 653 us
  waiting for transfers between devices  377 us (57%)
  matrix products  129 us (19%)
  starting transfers between devices  67.6 us (10%)
  other arithmetic  22.7 us (3%)
  local copies, waits for them, and re-layouts  22.3 us (3%)
  between operations  17.5 us (3%)
  Pallas kernels  16.8 us (3%)
    all_to_all x9, waiting for transfers between devices, swap(): return lax.all_to_all(x, axis, split_axis=0, concat_axis=0, tiled=True)  179 us
    dot_general x11, matrix products, dot32(): return jnp.dot(a, b, preferred_element_type=jnp.float32)  106 us
    ppermute x4, waiting for transfers between devices, reduce_sets(): came = [lax.ppermute(a, 'col', pairs) for a in away]  99.1 us
    all_gather x1, waiting for transfers between devices, body(): gathered = lax.all_gather(lmo_coef, 'row', axis=0, tiled=True)  52.5 us
    all_to_all x9, starting transfers between devices, swap(): return lax.all_to_all(x, axis, split_axis=0, concat_axis=0, tiled=True)  39.5 us
    ppermute x6, waiting for transfers between devices, hop(): return lax.ppermute(x.astype(jnp.bfloat16), 'col', perm).astype(jnp.float32)  37.1 us
    ppermute x6, starting transfers between devices, hop(): return lax.ppermute(x.astype(jnp.bfloat16), 'col', perm).astype(jnp.float32)  21.5 us
    pallas_call x7, Pallas kernels, pick(): pl.pallas_call(functools.partial(pick_kernel, count, width), out_shape=ja...  16.8 us
  transfers between devices with their start and end apart: 23, of which 16 were waited for; matrix products, arithmetic and copies ran while one was open for 23% of the time, Pallas kernels for 3%

profile of v3, /device:TPU:0, one launch (start us, length us, event | category | flops | bytes accessed | tf_op | source)
XLA Modules:
  0.0 652.8 jit_solution(5464462667524652458)
XLA Ops:
  26.8 52.5 %all-gather.2.cloned.1.call-done.src_ref = bf16[4096,1024]{1,0:T(8,128)(2,1)} async-done(((bf16[1024,1024]{1,0:T(8,128)(2,1)}), bf16[4096,1024]{1,0:T(8,128)(2,1)}) %all-gather.2.cloned.1.call-update) | async-done | bytes 8388624 | tf_op jit(solution)/shard_map/all_gather | solution.py:138
  79.2 14.6 %fusion.37 = bf16[1024,1024]{1,0:T(8,128)(2,1)S(1)} fusion(bf16[4096,1024]{1,0:T(8,128)(2,1)} %all-gather.2.cloned.1.call-done.src_ref, bf16[8192,1,4096]{2,0,1:T(8,128)(2,1)} %param.7, s32[]{:T(128)S(6)} %select_n.192), kind=kOutput, calls=%fused_computation.45 | convolution fusion | flops 8590983168 | bytes 18874372 | tf_op jit(solution)/shard_map/dot_general | solution.py:51
  96.0 12.2 %fusion.28 = bf16[1024,1024]{1,0:T(8,128)(2,1)} fusion(bf16[4096,1024]{1,0:T(8,128)(2,1)S(1)} %copy-done, bf16[8192,1,4096]{2,0,1:T(8,128)(2,1)} %param.7, s32[]{:T(128)S(6)} %select_n.183), kind=kOutput, calls=%fused_computation.42 | convolution fusion | flops 8590983168 | bytes 18874372 | tf_op jit(solution)/shard_map/dot_general | solution.py:51
  108.3 11.2 %fusion.31 = bf16[1024,1024]{1,0:T(8,128)(2,1)S(1)} fusion(bf16[4096,1024]{1,0:T(8,128)(2,1)S(1)} %copy-done, bf16[8192,1,4096]{2,0,1:T(8,128)(2,1)} %param.7, s32[]{:T(128)S(6)} %select_n.186), kind=kOutput, calls=%fused_computation.43 | convolution fusion | flops 8590983168 | bytes 18874372 | tf_op jit(solution)/shard_map/dot_general | solution.py:51
  121.5 12.6 %fusion.34 = bf16[1024,1024]{1,0:T(8,128)(2,1)} fusion(bf16[4096,1024]{1,0:T(8,128)(2,1)S(1)} %copy-done, bf16[8192,1,4096]{2,0,1:T(8,128)(2,1)} %param.7, s32[]{:T(128)S(6)} %select_n.188), kind=kOutput, calls=%fused_computation.44 | convolution fusion | flops 8590983168 | bytes 18874372 | tf_op jit(solution)/shard_map/dot_general | solution.py:51
  134.2 8.3 %collective-permute-done.3 = bf16[1024,1024]{1,0:T(8,128)(2,1)S(1)} collective-permute-done((bf16[1024,1024]{1,0:T(8,128)(2,1)S(1)}, bf16[1024,1024]{1,0:T(8,128)(2,1)S(1)}, u32[]{:S(2)}, u32[]{:S(2)}) %collective-permute-start.3) | collective-permute-done | bytes 2097184 | tf_op jit(solution)/shard_map/ppermute | solution.py:72
  142.4 11.2 %add_convert_fusion.5 = bf16[1024,1024]{1,0:T(8,128)(2,1)S(1)} fusion(bf16[1024,1024]{1,0:T(8,128)(2,1)S(1)} %collective-permute-done.3, bf16[4096,1024]{1,0:T(8,128)(2,1)S(1)} %copy-done, bf16[8192,1,4096]{2,0,1:T(8,128)(2,1)} %param.7, s32[]{:T(128)S(6)} %select_n.191), kind=kOutput, calls=%fused_computation.31 | convolution fusion | flops 8593080320 | bytes 20971524 | tf_op jit(solution)/shard_map/dot_general | solution.py:51
  158.6 73.7 %collective-permute-done.1 = bf16[1024,1024]{1,0:T(8,128)(2,1)S(1)} collective-permute-done((bf16[1024,1024]{1,0:T(8,128)(2,1)S(1)}, bf16[1024,1024]{1,0:T(8,128)(2,1)S(1)}, u32[]{:S(2)}, u32[]{:S(2)}) %collective-permute-start.1) | collective-permute-done | bytes 2097184 | tf_op jit(solution)/shard_map/ppermute | solution.py:72
  232.3 11.3 %add_convert_fusion.7 = bf16[1024,1024]{1,0:T(8,128)(2,1)S(1)} fusion(bf16[1024,1024]{1,0:T(8,128)(2,1)S(1)} %collective-permute-done.1, bf16[4096,1024]{1,0:T(8,128)(2,1)S(1)} %copy-done, bf16[8192,1,4096]{2,0,1:T(8,128)(2,1)} %param.7, s32[]{:T(128)S(6)} %select_n.185), kind=kOutput, calls=%fused_computation.33 | convolution fusion | flops 8593080320 | bytes 20971524 | tf_op jit(solution)/shard_map/dot_general | solution.py:51
  247.9 5.4 collective-permute-start.5
  259.8 17.2 %collective-permute-done.2 = bf16[1024,1024]{1,0:T(8,128)(2,1)} collective-permute-done((bf16[1024,1024]{1,0:T(8,128)(2,1)}, bf16[1024,1024]{1,0:T(8,128)(2,1)}, u32[]{:S(2)}, u32[]{:S(2)}) %collective-permute-start.2) | collective-permute-done | bytes 2097184 | tf_op jit(solution)/shard_map/ppermute | solution.py:72
  277.0 14.0 %add_convert_fusion.6 = bf16[1024,1024]{1,0:T(8,128)(2,1)S(1)} fusion(bf16[1024,1024]{1,0:T(8,128)(2,1)} %collective-permute-done.2, bf16[4096,1024]{1,0:T(8,128)(2,1)} %all-gather.2.cloned.1.call-done.src_ref, bf16[8192,1,4096]{2,0,1:T(8,128)(2,1)} %param.7, s32[]{:T(128)S(6)} %select_n.187), kind=kOutput, calls=%fused_computation.32 | convolution fusion | flops 8593080320 | bytes 20971524 | tf_op jit(solution)/shard_map/dot_general | solution.py:51
  296.1 6.4 add_convert_fusion.3
  302.5 7.8 %collective-permute-start.6 = (bf16[1024,1024]{1,0:T(8,128)(2,1)}, bf16[1024,1024]{1,0:T(8,128)(2,1)S(1)}, u32[]{:S(2)}, u32[]{:S(2)}) collective-permute-start(bf16[1024,1024]{1,0:T(8,128)(2,1)} %get-tuple-element.13), channel_id=1, source_target_pairs={{0,2},{1,3},{2,4},{3,5},{4,6},{5,7},{8,10},{9,11},{10,12},{11,13},... | collective-permute-start | bytes 6291464 | tf_op jit(solution)/shard_map/ppermute | solution.py:84
  320.3 12.6 %fusion.14 = f32[1024,1024]{1,0:T(8,128)S(1)} fusion(bf16[4096,1024]{1,0:T(8,128)(2,1)} %all-gather.2.cloned.1.call-done.src_ref, bf16[8192,1,4096]{2,0,1:T(8,128)(2,1)} %param.7, s32[]{:T(128)S(6)} %select_n.182), kind=kOutput, calls=%fused_computation.15 | convolution fusion | flops 8589934592 | bytes 20971524 | tf_op jit(solution)/shard_map/dot_general | solution.py:51
  332.9 23.6 %collective-permute-done.6 = bf16[1024,1024]{1,0:T(8,128)(2,1)S(1)} collective-permute-done((bf16[1024,1024]{1,0:T(8,128)(2,1)}, bf16[1024,1024]{1,0:T(8,128)(2,1)S(1)}, u32[]{:S(2)}, u32[]{:S(2)}) %collective-permute-start.6) | collective-permute-done | bytes 2097184 | tf_op jit(solution)/shard_map/ppermute | solution.py:84
  356.5 8.5 %collective-permute-done.9 = bf16[1024,1024]{1,0:T(8,128)(2,1)} collective-permute-done((bf16[1024,1024]{1,0:T(8,128)(2,1)}, bf16[1024,1024]{1,0:T(8,128)(2,1)}, u32[]{:S(2)}, u32[]{:S(2)}) %collective-permute-start.9) | collective-permute-done | bytes 2097184 | tf_op jit(solution)/shard_map/ppermute | solution.py:84
  388.3 45.1 %all-to-all-done.3 = bf16[4,512,1024]{2,1,0:T(8,128)(2,1)} async-done(((bf16[4,512,1024]{2,1,0:T(8,128)(2,1)}), bf16[4,512,1024]{2,1,0:T(8,128)(2,1)}, u32[]{:S(2)}, u32[]{:S(2)}) %all-to-all-start.3) | async-done | bytes 4194336 | tf_op jit(solution)/shard_map/all_to_all | solution.py:55
  441.5 44.6 %all-to-all-done.1 = bf16[8,8,128,128]{3,2,1,0:T(8,128)(2,1)} async-done(((bf16[8,8,128,128]{3,2,1,0:T(8,128)(2,1)}), bf16[8,8,128,128]{3,2,1,0:T(8,128)(2,1)}, u32[]{:S(2)}, u32[]{:S(2)}) %all-to-all-start.1) | async-done | bytes 2097184 | tf_op jit(solution)/shard_map/all_to_all | solution.py:55
  495.3 9.0 %all-to-all-done.5 = bf16[8,32,1024]{2,1,0:T(8,128)(2,1)S(1)} async-done(((bf16[8,32,1024]{2,1,0:T(8,128)(2,1)}), bf16[8,32,1024]{2,1,0:T(8,128)(2,1)S(1)}, u32[]{:S(2)}, u32[]{:S(2)}) %all-to-all-start.5) | async-done | bytes 524320 | tf_op jit(solution)/shard_map/all_to_all | solution.py:55
  508.8 47.7 %all-to-all-done.2 = bf16[8,128,1024]{2,1,0:T(8,128)(2,1)} async-done(((bf16[8,128,1024]{2,1,0:T(8,128)(2,1)}), bf16[8,128,1024]{2,1,0:T(8,128)(2,1)}, u32[]{:S(2)}, u32[]{:S(2)}) %all-to-all-start.2) | async-done | bytes 2097184 | tf_op jit(solution)/shard_map/all_to_all | solution.py:55
  563.8 12.0 %all-to-all-done.6 = bf16[8,32,1024]{2,1,0:T(8,128)(2,1)} async-done(((bf16[8,32,1024]{2,1,0:T(8,128)(2,1)}), bf16[8,32,1024]{2,1,0:T(8,128)(2,1)}, u32[]{:S(2)}, u32[]{:S(2)}) %all-to-all-start.6) | async-done | bytes 524320 | tf_op jit(solution)/shard_map/all_to_all | solution.py:55
  611.3 16.7 %all-to-all-done.4 = bf16[8,128,1024]{2,1,0:T(8,128)(2,1)} async-done(((bf16[8,128,1024]{2,1,0:T(8,128)(2,1)}), bf16[8,128,1024]{2,1,0:T(8,128)(2,1)}, u32[]{:S(2)}, u32[]{:S(2)}) %all-to-all-start.4) | async-done | bytes 2097184 | tf_op jit(solution)/shard_map/all_to_all | solution.py:55
  632.3 5.9 fusion.47
  (108 shorter events, 151.3 us)
Async XLA Ops:
  7.2 72.0 %all-gather.2.cloned.1.call-start = ((), (), s32[]{:S(2)}) async-start(), calls=%async_computation.9 | async-start | bytes 10485760 | tf_op jit(solution)/shard_map/all_gather | solution.py:138
  13.8 241.6 %all-to-all-start.7 = ((bf16[8,128,512]{2,1,0:T(8,128)(2,1)}), bf16[8,128,512]{2,1,0:T(8,128)(2,1)S(1)}, u32[]{:S(2)}, u32[]{:S(2)}) async-start(bf16[8,128,512]{2,1,0:T(8,128)(2,1)} %shard_map.91), calls=%async_computation.7 | async-start | bytes 2097152 | tf_op jit(solution)/shard_map/all_to_all | solution.py:55
  93.8 48.7 %collective-permute-start.3 = (bf16[1024,1024]{1,0:T(8,128)(2,1)S(1)}, bf16[1024,1024]{1,0:T(8,128)(2,1)S(1)}, u32[]{:S(2)}, u32[]{:S(2)}) collective-permute-start(bf16[1024,1024]{1,0:T(8,128)(2,1)S(1)} %fusion.37), channel_id=1, source_target_pairs={{0,1},{1,0},{2,3},{3,2},{4,5},{5,4},{6,7},{7,6},{8,9},{9,8},{10,11... | collective-permute-start | bytes 6291464 | tf_op jit(solution)/shard_map/ppermute | solution.py:72
  108.2 224.7 %collective-permute-start = (bf16[1024,1024]{1,0:T(8,128)(2,1)}, bf16[1024,1024]{1,0:T(8,128)(2,1)}, u32[]{:S(2)}, u32[]{:S(2)}) collective-permute-start(bf16[1024,1024]{1,0:T(8,128)(2,1)} %fusion.28), channel_id=1, source_target_pairs={{0,1},{1,0},{2,3},{3,2},{4,5},{5,4},{6,7},{7,6},{8,9},{9,8},{10,11... | collective-permute-start | bytes 6291464 | tf_op jit(solution)/shard_map/ppermute | solution.py:72
  119.5 112.9 %collective-permute-start.1 = (bf16[1024,1024]{1,0:T(8,128)(2,1)S(1)}, bf16[1024,1024]{1,0:T(8,128)(2,1)S(1)}, u32[]{:S(2)}, u32[]{:S(2)}) collective-permute-start(bf16[1024,1024]{1,0:T(8,128)(2,1)S(1)} %fusion.31), channel_id=1, source_target_pairs={{0,1},{1,0},{2,3},{3,2},{4,5},{5,4},{6,7},{7,6},{8,9},{9,8},{10,11... | collective-permute-start | bytes 6291464 | tf_op jit(solution)/shard_map/ppermute | solution.py:72
  134.1 142.9 %collective-permute-start.2 = (bf16[1024,1024]{1,0:T(8,128)(2,1)}, bf16[1024,1024]{1,0:T(8,128)(2,1)}, u32[]{:S(2)}, u32[]{:S(2)}) collective-permute-start(bf16[1024,1024]{1,0:T(8,128)(2,1)} %fusion.34), channel_id=1, source_target_pairs={{0,1},{1,0},{2,3},{3,2},{4,5},{5,4},{6,7},{7,6},{8,9},{9,8},{10,11... | collective-permute-start | bytes 6291464 | tf_op jit(solution)/shard_map/ppermute | solution.py:72
  153.6 90.0 %collective-permute-start.4 = (bf16[1024,1024]{1,0:T(8,128)(2,1)S(1)}, bf16[1024,1024]{1,0:T(8,128)(2,1)S(1)}, u32[]{:S(2)}, u32[]{:S(2)}) collective-permute-start(bf16[1024,1024]{1,0:T(8,128)(2,1)S(1)} %add_convert_fusion.5), channel_id=1, source_target_pairs={{0,2},{1,3},{8,10},{9,11},{16,18},{17,19},{24,26},{25,27}} | collective-permute-start | bytes 6291464 | tf_op jit(solution)/shard_map/ppermute | solution.py:84
  157.8 85.9 %collective-permute-start.7 = (bf16[1024,1024]{1,0:T(8,128)(2,1)S(1)}, bf16[1024,1024]{1,0:T(8,128)(2,1)S(1)}, u32[]{:S(2)}, u32[]{:S(2)}) collective-permute-start(bf16[1024,1024]{1,0:T(8,128)(2,1)S(1)} %add_convert_fusion.5), channel_id=1, source_target_pairs={{6,4},{7,5},{14,12},{15,13},{22,20},{23,21},{30,28},{31,29}} | collective-permute-start | bytes 6291464 | tf_op jit(solution)/shard_map/ppermute | solution.py:84
  247.9 48.2 %collective-permute-start.5 = (bf16[1024,1024]{1,0:T(8,128)(2,1)}, bf16[1024,1024]{1,0:T(8,128)(2,1)}, u32[]{:S(2)}, u32[]{:S(2)}) collective-permute-start(bf16[1024,1024]{1,0:T(8,128)(2,1)} %get-tuple-element.15), channel_id=1, source_target_pairs={{0,2},{1,3},{2,4},{3,5},{8,10},{9,11},{10,12},{11,13},{16,18},{17,... | collective-permute-start | bytes 6291464 | tf_op jit(solution)/shard_map/ppermute | solution.py:84
  253.3 42.8 %collective-permute-start.8 = (bf16[1024,1024]{1,0:T(8,128)(2,1)}, bf16[1024,1024]{1,0:T(8,128)(2,1)}, u32[]{:S(2)}, u32[]{:S(2)}) collective-permute-start(bf16[1024,1024]{1,0:T(8,128)(2,1)} %get-tuple-element.16), channel_id=1, source_target_pairs={{4,2},{5,3},{6,4},{7,5},{12,10},{13,11},{14,12},{15,13},{20,18},{2... | collective-permute-start | bytes 6291464 | tf_op jit(solution)/shard_map/ppermute | solution.py:84
  255.4 60.1 %all-to-all-start = ((bf16[4,8,2,128,128]{4,3,2,1,0:T(8,128)(2,1)}), bf16[4,8,2,128,128]{4,3,2,1,0:T(8,128)(2,1)}, u32[]{:S(2)}, u32[]{:S(2)}) async-start(bf16[4,8,2,128,128]{4,3,2,1,0:T(8,128)(2,1)} %bitcast.7), calls=%async_computation | async-start | bytes 4194304 | tf_op jit(solution)/shard_map/all_to_all | solution.py:55
  291.0 21.4 %copy-start.6 = (s32[8]{0:T(128)S(1)}, s32[8]{0:T(128)}, u32[]{:S(2)}) copy-start(s32[8]{0:T(128)} %copy-done.5) | copy-start | bytes 100
  302.5 54.0 %collective-permute-start.6 = (bf16[1024,1024]{1,0:T(8,128)(2,1)}, bf16[1024,1024]{1,0:T(8,128)(2,1)S(1)}, u32[]{:S(2)}, u32[]{:S(2)}) collective-permute-start(bf16[1024,1024]{1,0:T(8,128)(2,1)} %get-tuple-element.13), channel_id=1, source_target_pairs={{0,2},{1,3},{2,4},{3,5},{4,6},{5,7},{8,10},{9,11},{10,12},{11,13},... | collective-permute-start | bytes 6291464 | tf_op jit(solution)/shard_map/ppermute | solution.py:84
  310.2 54.7 %collective-permute-start.9 = (bf16[1024,1024]{1,0:T(8,128)(2,1)}, bf16[1024,1024]{1,0:T(8,128)(2,1)}, u32[]{:S(2)}, u32[]{:S(2)}) collective-permute-start(bf16[1024,1024]{1,0:T(8,128)(2,1)} %get-tuple-element.14), channel_id=1, source_target_pairs={{2,0},{3,1},{4,2},{5,3},{6,4},{7,5},{10,8},{11,9},{12,10},{13,11},... | collective-permute-start | bytes 6291464 | tf_op jit(solution)/shard_map/ppermute | solution.py:84
  315.5 63.8 %all-to-all-start.8 = ((bf16[8,128,512]{2,1,0:T(8,128)(2,1)}), bf16[8,128,512]{2,1,0:T(8,128)(2,1)S(1)}, u32[]{:S(2)}, u32[]{:S(2)}) async-start(bf16[8,128,512]{2,1,0:T(8,128)(2,1)} %shard_map.92), calls=%async_computation.8 | async-start | bytes 2097152 | tf_op jit(solution)/shard_map/all_to_all | solution.py:55
  380.2 53.1 %all-to-all-start.3 = ((bf16[4,512,1024]{2,1,0:T(8,128)(2,1)}), bf16[4,512,1024]{2,1,0:T(8,128)(2,1)}, u32[]{:S(2)}, u32[]{:S(2)}) async-start(bf16[4,512,1024]{2,1,0:T(8,128)(2,1)} %pad_maximum_fusion), calls=%async_computation.3 | async-start | bytes 8388608 | tf_op jit(solution)/shard_map/all_to_all | solution.py:55
  433.4 52.7 %all-to-all-start.1 = ((bf16[8,8,128,128]{3,2,1,0:T(8,128)(2,1)}), bf16[8,8,128,128]{3,2,1,0:T(8,128)(2,1)}, u32[]{:S(2)}, u32[]{:S(2)}) async-start(bf16[8,8,128,128]{3,2,1,0:T(8,128)(2,1)} %bitcast.9), calls=%async_computation.1 | async-start | bytes 4194304 | tf_op jit(solution)/shard_map/all_to_all | solution.py:55
  486.1 18.3 %all-to-all-start.5 = ((bf16[8,32,1024]{2,1,0:T(8,128)(2,1)}), bf16[8,32,1024]{2,1,0:T(8,128)(2,1)S(1)}, u32[]{:S(2)}, u32[]{:S(2)}) async-start(bf16[8,32,1024]{2,1,0:T(8,128)(2,1)} %bitcast.33), calls=%async_computation.5 | async-start | bytes 1048576 | tf_op jit(solution)/shard_map/all_to_all | solution.py:55
  504.3 52.2 %all-to-all-start.2 = ((bf16[8,128,1024]{2,1,0:T(8,128)(2,1)}), bf16[8,128,1024]{2,1,0:T(8,128)(2,1)}, u32[]{:S(2)}, u32[]{:S(2)}) async-start(bf16[8,128,1024]{2,1,0:T(8,128)(2,1)} %copy-done.2), calls=%async_computation.2 | async-start | bytes 4194304 | tf_op jit(solution)/shard_map/all_to_all | solution.py:55
  557.4 18.4 %all-to-all-start.6 = ((bf16[8,32,1024]{2,1,0:T(8,128)(2,1)}), bf16[8,32,1024]{2,1,0:T(8,128)(2,1)}, u32[]{:S(2)}, u32[]{:S(2)}) async-start(bf16[8,32,1024]{2,1,0:T(8,128)(2,1)} %broadcast_in_dim.90), calls=%async_computation.6 | async-start | bytes 1048576 | tf_op jit(solution)/shard_map/all_to_all | solution.py:55
  575.8 52.2 %all-to-all-start.4 = ((bf16[8,128,1024]{2,1,0:T(8,128)(2,1)}), bf16[8,128,1024]{2,1,0:T(8,128)(2,1)}, u32[]{:S(2)}, u32[]{:S(2)}) async-start(bf16[8,128,1024]{2,1,0:T(8,128)(2,1)} %shard_map.90), calls=%async_computation.4 | async-start | bytes 4194304 | tf_op jit(solution)/shard_map/all_to_all | solution.py:55
  591.5 10.9 %collective-permute-start.10 = (bf16[256,1024]{1,0:T(8,128)(2,1)}, bf16[256,1024]{1,0:T(8,128)(2,1)S(1)}, u32[]{:S(2)}, u32[]{:S(2)}) collective-permute-start(bf16[256,1024]{1,0:T(8,128)(2,1)} %bitcast.34), channel_id=1, source_target_pairs={{0,8},{8,16},{16,24},{24,0},{1,9},{9,17},{17,25},{25,1},{2,10},{10... | collective-permute-start | bytes 1572872 | tf_op jit(solution)/shard_map/ppermute | solution.py:165
  594.3 15.1 %collective-permute-start.11 = (bf16[256,1024]{1,0:T(8,128)(2,1)}, bf16[256,1024]{1,0:T(8,128)(2,1)S(1)}, u32[]{:S(2)}, u32[]{:S(2)}) collective-permute-start(bf16[256,1024]{1,0:T(8,128)(2,1)} %bitcast.34), channel_id=1, source_target_pairs={{0,16},{8,24},{16,0},{24,8},{1,17},{9,25},{17,1},{25,9},{2,18},{10... | collective-permute-start | bytes 1572872 | tf_op jit(solution)/shard_map/ppermute | solution.py:165
  595.0 37.3 %collective-permute-start.12 = (bf16[256,1024]{1,0:T(8,128)(2,1)}, bf16[256,1024]{1,0:T(8,128)(2,1)}, u32[]{:S(2)}, u32[]{:S(2)}) collective-permute-start(bf16[256,1024]{1,0:T(8,128)(2,1)} %bitcast.34), channel_id=1, source_target_pairs={{0,24},{8,0},{16,8},{24,16},{1,25},{9,1},{17,9},{25,17},{2,26},{10... | collective-permute-start | bytes 1572872 | tf_op jit(solution)/shard_map/ppermute | solution.py:165
  (13 other events, 55.0 us)
Sparse Core Ops, SparseCore 0:
  9.6 69.5 all-gather.1
